TPU v7x, 32 devices: a whole 2x2x4 slice. The times are simulated.
32 devices in a mesh: dp: 2 (over y), row: 4 (over z), col: 4 (over x, core).
Axes of the slice: x: 2, y: 2, z: 4, core: 2. Of those that a mesh axis runs over, the one named last changes fastest.
Arguments:
- images_in: bfloat16 [8, 64, 64, 1024], P('dp', 'row', 'col'), may hold values from -6 to 6
- keep: int32 [8], P('dp'), may hold values from 0 to 1, as said below
- dw_weight: bfloat16 [49, 1024], replicated, may hold values from -0.875 to 0.875
- layer_norm_gain: float32 [1024], replicated, may hold values from 0.25 to 1.75
- w_in: bfloat16 [1024, 2048], replicated, may hold values from -0.1875 to 0.1875
- w_out: bfloat16 [2048, 1024], replicated, may hold values from -0.125 to 0.125
- layer_scale: float32 [1024], replicated, may hold values from 0.25 to 1
- out_grad: bfloat16 [8, 64, 64, 1024], P('dp', 'row', 'col'), may hold values from -6 to 6
Outputs:
- output: bfloat16 [8, 64, 64, 1024], P('dp', 'row', 'col')
- grad_input: bfloat16 [8, 64, 64, 1024], P('dp', 'row', 'col')
- grad_w_in: float32 [1024, 2048], P(('dp', 'row', 'col'))
- grad_w_out: float32 [2048, 1024], P(('dp', 'row', 'col'))
- grad_dw: float32 [49, 1024], replicated
- grad_ln_gain: float32 [1024], replicated
- grad_layer_scale: float32 [1024], replicated
Inputs may be any that keep to these rules, and one draw needn't show every extreme that they name: `keep`: 1 keeps the image's residual branch, 0 drops it; at least one and at most 4 images are dropped.
All inputs are finite; a program needn't handle non-finite values.
Results may differ from a plain program's by a relative error of at most 0.0062.
Values may be sent and summed in bfloat16 or wider, within the bound.
A program may use at most 128 MiB of HBM per device.

v0:
```python
import math

import jax
import jax.numpy as jnp
from jax import lax
from jax.sharding import PartitionSpec as P

KERNEL = 7


eps = 1e-06
keep_rate = 0.75


def extended(block, sides, width):
    for axis, dim in sides:
        count = lax.axis_size(axis)
        forward = [(i, i + 1) for i in range(count - 1)]
        backward = [(target, source) for source, target in forward]
        low = lax.ppermute(
            lax.slice_in_dim(block, block.shape[dim] - width, None, axis=dim), axis, forward
        )
        high = lax.ppermute(lax.slice_in_dim(block, 0, width, axis=dim), axis, backward)
        block = jnp.concatenate([low, block, high], axis=dim)
    return block


def depthwise(padded, kernel, width):
    taps = kernel.reshape(KERNEL, KERNEL, 1, width)
    return lax.conv_general_dilated(
        padded,
        taps,
        (1, 1),
        "VALID",
        dimension_numbers=("NHWC", "HWIO", "NHWC"),
        feature_group_count=width,
        preferred_element_type=jnp.float32,
    )


def extend(field):
    return extended(field, (("row", 1), ("col", 2)), KERNEL // 2)


def shards(images_in, keep, dw_weight, layer_norm_gain, w_in, w_out, layer_scale, out_grad):
    batch, tile_h, tile_w, width = images_in.shape
    cells = tile_h * tile_w
    total_rows = batch * cells
    padded = extend(images_in)
    conv = depthwise(padded, dw_weight, width).reshape(total_rows, width)
    mean_v = jnp.mean(conv, axis=-1, keepdims=True)
    local_device = conv - mean_v
    inverse_deviation = lax.rsqrt(
        jnp.mean(local_device * local_device, axis=-1, keepdims=True) + eps
    )
    centered_scaled_input = local_device * inverse_deviation
    normalized_input = (centered_scaled_input * layer_norm_gain).astype(jnp.bfloat16)
    pre = jnp.dot(normalized_input, w_in, preferred_element_type=jnp.float32)
    cdf = 0.5 * (1.0 + lax.erf(pre * (1.0 / math.sqrt(2.0))))
    hidden = (pre * cdf).astype(jnp.bfloat16)
    branch = jnp.dot(hidden, w_out, preferred_element_type=jnp.float32)
    factor = jnp.repeat(keep.astype(jnp.float32) / keep_rate, cells)[:, None]
    flat_in = images_in.reshape(total_rows, width).astype(jnp.float32)
    output = (flat_in + factor * layer_scale * branch).astype(jnp.bfloat16).reshape(images_in.shape)
    upstream = out_grad.reshape(total_rows, width).astype(jnp.float32)
    g_branch = (factor * layer_scale * upstream).astype(jnp.bfloat16)
    gamma_term = jnp.sum(factor * upstream * branch, axis=0)
    slope = cdf + pre * jnp.exp(-0.5 * pre * pre) * (1.0 / math.sqrt(2.0 * math.pi))
    g_pre = (jnp.dot(g_branch, w_out.T, preferred_element_type=jnp.float32) * slope).astype(
        jnp.bfloat16
    )
    normalized_gradient = jnp.dot(g_pre, w_in.T, preferred_element_type=jnp.float32)
    gain_contribution = jnp.sum(normalized_gradient * centered_scaled_input, axis=0)
    input_gradient = normalized_gradient * layer_norm_gain
    convolution_gradient = (
        inverse_deviation
        * (
            input_gradient
            - jnp.mean(input_gradient, axis=-1, keepdims=True)
            - centered_scaled_input
            * jnp.mean(input_gradient * centered_scaled_input, axis=-1, keepdims=True)
        )
    ).astype(jnp.bfloat16)
    g_conv4 = convolution_gradient.reshape(batch, tile_h, tile_w, width)
    g_wide = g_conv4.astype(jnp.float32)
    dw_terms = []
    for i in range(KERNEL):
        for j in range(KERNEL):
            window = padded[:, i : i + tile_h, j : j + tile_w, :].astype(jnp.float32)
            dw_terms.append(jnp.sum(g_wide * window, axis=(0, 1, 2)))
    dw_term = jnp.stack(dw_terms, axis=0)
    flipped = dw_weight.reshape(KERNEL, KERNEL, width)[::-1, ::-1].reshape(KERNEL * KERNEL, width)
    back = depthwise(extend(g_conv4), flipped, width).reshape(total_rows, width)
    grad_input = (upstream + back).astype(jnp.bfloat16).reshape(images_in.shape)
    images = jnp.float32(batch * lax.axis_size("dp"))
    dw_sum, gain_sum, gamma_sum = lax.psum(
        (dw_term, gain_contribution, gamma_term), ("dp", "row", "col")
    )
    w_in_term = jnp.dot(normalized_input.T, g_pre, preferred_element_type=jnp.float32)
    w_out_term = jnp.dot(hidden.T, g_branch, preferred_element_type=jnp.float32)
    w_in_sum, w_out_sum = (
        lax.psum_scatter(w_in_term, ("dp", "row", "col"), scatter_dimension=0, tiled=True),
        lax.psum_scatter(w_out_term, ("dp", "row", "col"), scatter_dimension=0, tiled=True),
    )
    return (
        output,
        grad_input,
        w_in_sum / images,
        w_out_sum / images,
        dw_sum / images,
        gain_sum / images,
        gamma_sum / images,
    )


def solution(mesh):
    placed = (
        P("dp", "row", "col", None),
        P("dp"),
        P(),
        P(),
        P(),
        P(),
        P(),
        P("dp", "row", "col", None),
    )
    return jax.shard_map(
        shards,
        mesh=mesh,
        in_specs=placed,
        out_specs=(
            P("dp", "row", "col", None),
            P("dp", "row", "col", None),
            P(("dp", "row", "col"), None),
            P(("dp", "row", "col"), None),
            P(),
            P(),
            P(),
        ),
        check_vma=False,
    )
```

profile of v0, /device:TPU:0, one launch (start us, length us, event | category | flops | bytes accessed | tf_op | source)
XLA Modules:
  0.0 645.2 jit_solution(5006209415736164986)
XLA Ops:
  8.9 5.0 collective-permute-start
  15.5 6.7 %collective-permute-done = bf16[4,3,16,1024]{3,0,2,1:T(4,128)(2,1)S(1)} collective-permute-done((bf16[4,3,16,1024]{3,0,2,1:T(4,128)(2,1)S(1)}, bf16[4,3,16,1024]{3,0,2,1:T(4,128)(2,1)S(1)}, u32[]{:S(2)}, u32[]{:S(2)}) %collective-permute-start) | collective-permute-done | bytes 393248 | tf_op jit(solution)/shard_map/ppermute | solution.py:20
  22.5 4.3 constant_dynamic-update-slice_fusion.6
  34.1 4.2 copy_convert_fusion
  39.1 6.7 %copy.73 = f32[4,16,16,1024]{3,2,1,0:T(8,128)} copy(f32[4,16,16,1024]{3,0,2,1:T(4,128)} %copy_convert_fusion) | data formatting | bytes 8388608 | tf_op jit(solution)/shard_map/convert_element_type | solution.py:65
  46.5 4.4 copy.63
  50.9 25.6 %fusion.122 = (f32[4,16,16]{0,2,1:T(8,128)S(1)}, f32[4,16,16,1024]{3,0,2,1:T(4,128)}) fusion(bf16[7,7,1,1024]{3,2,1,0:T(2,128)(2,1)S(1)} %copy-done.19, bf16[4,22,3,1024]{3,0,2,1:T(4,128)(2,1)S(1)} %collective-permute-done.3, bf16[4,22,16,1024]{3,0,2,1:T(4,128)(2,1)S(1)} %get-tuple-element.113, bf16[4,22,3,1024]{3,0,2,1:T(4,128)(2,1)} %collective-permute-done.2), kind=kOutput, calls=%fused_computation.248 | convolution fusion | flops 115702784 | bytes 8263680 | tf_op jit(solution)/shard_map/conv_general_dilated | solution.py:30
  76.9 6.7 %copy.68 = f32[4,16,16,1024]{3,2,1,0:T(8,128)} copy(f32[4,16,16,1024]{3,0,2,1:T(4,128)} %get-tuple-element.115) | data formatting | bytes 8388608 | tf_op jit(solution)/shard_map/conv_general_dilated | solution.py:30
  85.3 2.9 multiply_convert_fusion.2
  88.8 7.0 %multiply_convert_fusion = (bf16[1024,2048]{1,0:T(8,128)(2,1)S(1)}, f32[1024,2048]{1,0:T(8,128)}) fusion(bf16[1024,1024]{1,0:T(8,128)(2,1)S(1)} %multiply_convert_fusion.2, bf16[1024,2048]{1,0:T(8,128)(2,1)S(1)} %copy-done.23), kind=kOutput, calls=%fused_computation.96 | convolution fusion | flops 4305453056 | bytes 18874368 | tf_op jit(solution)/shard_map/dot_general | solution.py:58
  98.2 6.8 %fusion.59 = (f32[1024]{0:T(1024)S(1)}, bf16[1024,1024]{1,0:T(8,128)(2,1)S(1)}, bf16[1024,1024]{1,0:T(8,128)(2,1)}) fusion(f32[4,16,16,1024]{3,2,1,0:T(8,128)S(1)} %copy-done.11, f32[1024]{0:T(1024)S(1)} %bitcast.150, f32[1024]{0:T(1024)S(1)} %copy-done.24, f32[4,16,16,1024]{3,2,1,0:T(8,128)S(1)} %copy-done.12, ...), kind=kOutput, calls=%fused_computation.154 | convolution fusion | flops 4304403456 | bytes 20983808 | tf_op jit(solution)/shard_map/dot_general | solution.py:61
  105.0 9.9 %fusion.5 = bf16[1024,2048]{1,0:T(8,128)(2,1)S(1)} fusion(f32[1024,2048]{1,0:T(8,128)} %get-tuple-element.117, bf16[1024,1024]{1,0:T(8,128)(2,1)S(1)} %get-tuple-element.96, bf16[2048,1024]{1,0:T(8,128)(2,1)S(1)} %copy-done.22), kind=kOutput, calls=%fused_computation.95 | convolution fusion | flops 4315938816 | bytes 18874368 | tf_op jit(solution)/shard_map/dot_general | solution.py:69
  114.9 5.1 multiply_reduce_fusion
  122.5 8.2 %fusion.54 = (f32[1024]{0:T(1024)S(1)}, f32[1024]{0:T(1024)S(1)}, f32[1024]{0:T(1024)S(1)}, f32[1024]{0:T(1024)S(1)}, f32[1024]{0:T(1024)S(1)}, /*index=5*/f32[1024]{0:T(1024)S(1)}) fusion(bf16[4,19,16,1024]{3,0,2,1:T(4,128)(2,1)S(1)} %copy-done.4, bf16[4,16,16,1024]{3,2,1,0:T(8,128)(2,1)S(1)} %bitcast.90, bf16[4,19,16,1024]{3,0,2,1:T(4,128)(2,1)S(1)} %copy-done.6), kind=kLoop, calls=%fused_computation.148 | loop fusion | flops 19916800 | bytes 14704640 | tf_op jit(solution)/shard_map/reduce_sum | solution.py:90
  130.7 10.7 %fusion.50 = (f32[1024]{0:T(1024)S(1)}, f32[1024]{0:T(1024)S(1)}, f32[1024]{0:T(1024)S(1)}, f32[1024]{0:T(1024)S(1)}, f32[1024]{0:T(1024)S(1)}, /*index=5*/f32[1024]{0:T(1024)S(1)}) fusion(bf16[4,22,3,1024]{3,0,2,1:T(4,128)(2,1)S(1)} %collective-permute-done.3, bf16[4,22,16,1024]{3,0,2,1:T(4,128)(2,1)S(1)} %copy-done.1, ...), kind=kLoop, calls=%fused_computation.144 | loop fusion | flops 26208256 | bytes 6086656 | tf_op jit(solution)/shard_map/reduce_sum | solution.py:90
  141.4 9.7 %fusion.55 = (f32[1024]{0:T(1024)S(1)}, f32[1024]{0:T(1024)S(1)}, f32[1024]{0:T(1024)S(1)}, f32[1024]{0:T(1024)S(1)}, f32[1024]{0:T(1024)S(1)}, /*index=5*/f32[1024]{0:T(1024)S(1)}) fusion(bf16[4,22,3,1024]{3,0,2,1:T(4,128)(2,1)S(1)} %collective-permute-done.3, bf16[4,22,16,1024]{3,0,2,1:T(4,128)(2,1)S(1)} %copy-done.1, ...), kind=kLoop, calls=%fused_computation.149 | loop fusion | flops 26208256 | bytes 5545984 | tf_op jit(solution)/shard_map/reduce_sum | solution.py:90
  151.1 10.8 %fusion.51 = (f32[1024]{0:T(1024)S(1)}, f32[1024]{0:T(1024)S(1)}, f32[1024]{0:T(1024)S(1)}, f32[1024]{0:T(1024)S(1)}, f32[1024]{0:T(1024)S(1)}, /*index=5*/f32[1024]{0:T(1024)S(1)}) fusion(bf16[4,22,3,1024]{3,0,2,1:T(4,128)(2,1)} %collective-permute-done.2, bf16[4,22,16,1024]{3,0,2,1:T(4,128)(2,1)S(1)} %copy-done.1, bf16[4,16,16,1024]{3,2,1,0:T(8,128)(2,1)S(1)} %bitcast.93), kind=kLoop, calls=%fused_computation.145 | loop fusion | flops 26208256 | bytes 5545984 | tf_op jit(solution)/shard_map/reduce_sum | solution.py:90
  161.9 10.1 %fusion.56 = (f32[1024]{0:T(1024)S(1)}, f32[1024]{0:T(1024)S(1)}, f32[1024]{0:T(1024)S(1)}, f32[1024]{0:T(1024)S(1)}, f32[1024]{0:T(1024)S(1)}, /*index=5*/f32[1024]{0:T(1024)S(1)}) fusion(bf16[4,22,3,1024]{3,0,2,1:T(4,128)(2,1)S(1)} %collective-permute-done.3, bf16[4,22,16,1024]{3,0,2,1:T(4,128)(2,1)S(1)} %copy-done.1, ...), kind=kLoop, calls=%fused_computation.150 | loop fusion | flops 26208256 | bytes 5545984 | tf_op jit(solution)/shard_map/reduce_sum | solution.py:90
  172.0 10.9 %fusion.52 = (f32[1024]{0:T(1024)S(1)}, f32[1024]{0:T(1024)S(1)}, f32[1024]{0:T(1024)S(1)}, f32[1024]{0:T(1024)S(1)}, f32[1024]{0:T(1024)S(1)}, /*index=5*/f32[1024]{0:T(1024)S(1)}) fusion(bf16[4,22,3,1024]{3,0,2,1:T(4,128)(2,1)} %collective-permute-done.2, bf16[4,22,16,1024]{3,0,2,1:T(4,128)(2,1)S(1)} %copy-done.1, bf16[4,16,16,1024]{3,2,1,0:T(8,128)(2,1)S(1)} %bitcast.95), kind=kLoop, calls=%fused_computation.146 | loop fusion | flops 26208256 | bytes 5545984 | tf_op jit(solution)/shard_map/reduce_sum | solution.py:90
  182.9 11.6 %fusion.57 = (f32[1024]{0:T(1024)S(1)}, f32[1024]{0:T(1024)S(1)}, f32[1024]{0:T(1024)S(1)}, f32[1024]{0:T(1024)S(1)}, f32[1024]{0:T(1024)S(1)}, /*index=5*/f32[1024]{0:T(1024)S(1)}, f32[1024]{0:T(1024)S(1)}) fusion(bf16[4,22,3,1024]{3,0,2,1:T(4,128)(2,1)S(1)} %collective-permute-done.3, bf16[4,22,16,1024]{3,0,2,1:T(4,128)(2,1)S(1)} %copy-done.1, ...), kind=kLoop, calls=%fused_computation.151 | loop fusion | flops 29352960 | bytes 7647232 | tf_op jit(solution)/shard_map/reduce_sum | solution.py:90
  194.5 10.8 %fusion.53 = (f32[1024]{0:T(1024)S(1)}, f32[1024]{0:T(1024)S(1)}, f32[1024]{0:T(1024)S(1)}, f32[1024]{0:T(1024)S(1)}, f32[1024]{0:T(1024)S(1)}, /*index=5*/f32[1024]{0:T(1024)S(1)}) fusion(bf16[4,22,16,1024]{3,0,2,1:T(4,128)(2,1)S(1)} %copy-done.1, bf16[4,22,3,1024]{3,0,2,1:T(4,128)(2,1)} %collective-permute-done.2, bf16[4,16,16,1024]{3,2,1,0:T(8,128)(2,1)S(1)} %bitcast.97), kind=kLoop, calls=%fused_computation.147 | loop fusion | flops 26208256 | bytes 5545984 | tf_op jit(solution)/shard_map/reduce_sum | solution.py:90
  205.3 4.6 stack.199
  210.0 10.7 %fusion.124 = f32[2048,1024]{1,0:T(8,128)} fusion(bf16[1024,2048]{1,0:T(8,128)(2,1)} %copy-done.27, bf16[1024,1024]{1,0:T(8,128)(2,1)} %copy-done.28), kind=kOutput, calls=%fused_computation.250 | convolution fusion | flops 4294967296 | bytes 14680064 | tf_op jit(solution)/shard_map/dot_general | solution.py:100
  221.0 10.6 %fusion.123 = f32[1024,2048]{1,0:T(8,128)} fusion(bf16[1024,1024]{1,0:T(8,128)(2,1)} %copy-done.15, bf16[1024,2048]{1,0:T(8,128)(2,1)} %copy-done.26), kind=kOutput, calls=%fused_computation.249 | convolution fusion | flops 4294967296 | bytes 14680064 | tf_op jit(solution)/shard_map/dot_general | solution.py:99
  232.0 4.4 collective-permute-start.4
  238.0 7.0 %collective-permute-done.4 = bf16[4,3,16,1024]{3,0,2,1:T(4,128)(2,1)S(1)} collective-permute-done((bf16[4,3,16,1024]{3,0,2,1:T(4,128)(2,1)S(1)}, bf16[4,3,16,1024]{3,0,2,1:T(4,128)(2,1)S(1)}, u32[]{:S(2)}, u32[]{:S(2)}) %collective-permute-start.4) | collective-permute-done | bytes 393248 | tf_op jit(solution)/shard_map/ppermute | solution.py:20
  252.0 3.4 collective-permute-start.6
  257.1 43.0 %all-reduce = (f32[1024]{0:T(1024)S(1)}, f32[1024]{0:T(1024)S(1)}) all-reduce(f32[1024]{0:T(1024)S(1)} %get-tuple-element.35, f32[1024]{0:T(1024)S(1)} %get-tuple-element.95), channel_id=1, replica_groups=mesh['dp'=2,'row'=4,'col'=4] {'dp','row','col'}, use_global_device_ids=true, to_apply=%region_57.0 | all-reduce | flops 2048 | bytes 16384 | tf_op jit(solution)/shard_map/psum | solution.py:96
  300.7 37.0 %all-reduce.3.cloned.1.call-done = f32[49,1024]{1,0:T(8,128)} async-done(((f32[49,1024]{1,0:T(8,128)}), f32[49,1024]{1,0:T(8,128)}) %all-reduce.3.cloned.1.call-update) | async-done | bytes 200720 | tf_op jit(solution)/shard_map/psum | solution.py:96
  339.4 24.3 %add_convert_fusion = bf16[4,16,16,1024]{3,0,2,1:T(4,128)(2,1)S(1)} fusion(bf16[4,22,3,1024]{3,0,2,1:T(4,128)(2,1)} %collective-permute-done.7, bf16[4,22,16,1024]{3,0,2,1:T(4,128)(2,1)} %copy-done.16, bf16[4,22,3,1024]{3,0,2,1:T(4,128)(2,1)} %collective-permute-done.6, bf16[4,16,16,1024]{3,2,1,0:T(8,128)(2,1)S(1)} %copy-done.14, ...), kind=kOutput, calls=%fused_computation.158 | convolution fusion | flops 117800960 | bytes 8259584 | tf_op jit(solution)/shard_map/conv_general_dilated | solution.py:30
  365.6 123.5 %reduce-scatter.5.cloned.1.call-done = f32[64,1024]{1,0:T(8,128)} async-done(((f32[2048,1024]{1,0:T(8,128)}), f32[64,1024]{1,0:T(8,128)}) %reduce-scatter.5.cloned.1.call-update) | async-done | bytes 262160 | tf_op jit(solution)/shard_map/reduce_scatter | solution.py:103
  490.8 145.8 %reduce-scatter.3.cloned.1.call-done = f32[32,2048]{1,0:T(8,128)} async-done(((f32[1024,2048]{1,0:T(8,128)}), f32[32,2048]{1,0:T(8,128)}) %reduce-scatter.3.cloned.1.call-update) | async-done | bytes 262160 | tf_op jit(solution)/shard_map/reduce_scatter | solution.py:102
  (109 shorter events, 38.3 us)
Async XLA Ops:
  7.2 330.5 %all-reduce.3.cloned.1.call-start = ((), (), s32[]{:S(2)}) async-start(), calls=%async_computation.4 | async-start | bytes 458752 | tf_op jit(solution)/shard_map/psum | solution.py:96
  7.2 15.3 %copy-start.9 = (bf16[4,16,16,1024]{3,2,1,0:T(8,128)(2,1)S(1)}, bf16[4,16,16,1024]{3,2,1,0:T(8,128)(2,1)}, u32[]{:S(2)}) copy-start(bf16[4,16,16,1024]{3,2,1,0:T(8,128)(2,1)} %param.8) | copy-start | bytes 6291460
  8.9 13.3 %collective-permute-start = (bf16[4,3,16,1024]{3,0,2,1:T(4,128)(2,1)S(1)}, bf16[4,3,16,1024]{3,0,2,1:T(4,128)(2,1)S(1)}, u32[]{:S(2)}, u32[]{:S(2)}) collective-permute-start(bf16[4,3,16,1024]{3,0,2,1:T(4,128)(2,1)S(1)} %copy.143), channel_id=1, source_target_pairs={{0,4},{4,8},{8,12},{1,5},{5,9},{9,13},{2,6},{6,10},{10,14},{3,7},{... | collective-permute-start | bytes 1179656 | tf_op jit(solution)/shard_map/ppermute | solution.py:20
  14.2 12.6 %collective-permute-start.1 = (bf16[4,3,16,1024]{3,0,2,1:T(4,128)(2,1)S(1)}, bf16[4,3,16,1024]{3,0,2,1:T(4,128)(2,1)S(1)}, u32[]{:S(2)}, u32[]{:S(2)}) collective-permute-start(bf16[4,3,16,1024]{3,0,2,1:T(4,128)(2,1)S(1)} %copy.144), channel_id=1, source_target_pairs={{4,0},{8,4},{12,8},{5,1},{9,5},{13,9},{6,2},{10,6},{14,10},{7,3},{... | collective-permute-start | bytes 1179656 | tf_op jit(solution)/shard_map/ppermute | solution.py:23
  26.7 7.3 %copy-start.13 = (bf16[4,16,16,1024]{3,2,1,0:T(8,128)(2,1)S(1)}, bf16[4,16,16,1024]{3,2,1,0:T(8,128)(2,1)}, u32[]{:S(2)}) copy-start(bf16[4,16,16,1024]{3,2,1,0:T(8,128)(2,1)} %param.15) | copy-start | bytes 6291460
  28.6 22.4 %copy-start = (bf16[4,22,16,1024]{3,0,2,1:T(4,128)(2,1)}, bf16[4,22,16,1024]{3,0,2,1:T(4,128)(2,1)S(1)}, u32[]{:S(2)}) copy-start(bf16[4,22,16,1024]{3,0,2,1:T(4,128)(2,1)S(1)} %get-tuple-element.113) | copy-start | bytes 8650756
  30.6 7.8 %copy-start.17 = (bf16[49,1024]{1,0:T(8,128)(2,1)S(1)}, bf16[49,1024]{1,0:T(8,128)(2,1)}, u32[]{:S(2)}) copy-start(bf16[49,1024]{1,0:T(8,128)(2,1)} %param.10) | copy-start | bytes 301060
  30.6 20.3 %collective-permute-start.2 = (bf16[4,22,3,1024]{3,0,2,1:T(4,128)(2,1)}, bf16[4,22,3,1024]{3,0,2,1:T(4,128)(2,1)}, u32[]{:S(2)}, u32[]{:S(2)}) collective-permute-start(bf16[4,22,3,1024]{3,0,2,1:T(4,128)(2,1)} %get-tuple-element.100), channel_id=1, source_target_pairs={{0,1},{1,2},{2,3},{4,5},{5,6},{6,7},{8,9},{9,10},{10,11},{12,13},{... | collective-permute-start | bytes 1622024 | tf_op jit(solution)/shard_map/ppermute | solution.py:20
  32.8 18.1 %collective-permute-start.3 = (bf16[4,22,3,1024]{3,0,2,1:T(4,128)(2,1)}, bf16[4,22,3,1024]{3,0,2,1:T(4,128)(2,1)S(1)}, u32[]{:S(2)}, u32[]{:S(2)}) collective-permute-start(bf16[4,22,3,1024]{3,0,2,1:T(4,128)(2,1)} %get-tuple-element.101), channel_id=1, source_target_pairs={{1,0},{2,1},{3,2},{5,4},{6,5},{7,6},{9,8},{10,9},{11,10},{13,12},{... | collective-permute-start | bytes 1622024 | tf_op jit(solution)/shard_map/ppermute | solution.py:23
  39.1 6.7 %copy-start.25 = (s32[4]{0:T(128)S(1)}, s32[4]{0:T(128)}, u32[]{:S(2)}) copy-start(s32[4]{0:T(128)} %param.9) | copy-start | bytes 52
  39.1 7.4 %copy-start.7 = (f32[4,16,16,1024]{3,0,2,1:T(4,128)S(1)}, f32[4,16,16,1024]{3,0,2,1:T(4,128)}, u32[]{:S(2)}) copy-start(f32[4,16,16,1024]{3,0,2,1:T(4,128)} %get-tuple-element.103) | copy-start | bytes 12582916
  76.9 6.7 %copy-start.8 = (f32[4,16,16,1024]{3,0,2,1:T(4,128)S(1)}, f32[4,16,16,1024]{3,0,2,1:T(4,128)}, u32[]{:S(2)}) copy-start(f32[4,16,16,1024]{3,0,2,1:T(4,128)} %get-tuple-element.115) | copy-start | bytes 12582916
  88.7 7.0 %copy-start.15 = (bf16[1024,1024]{1,0:T(8,128)(2,1)}, bf16[1024,1024]{1,0:T(8,128)(2,1)S(1)}, u32[]{:S(2)}) copy-start(bf16[1024,1024]{1,0:T(8,128)(2,1)S(1)} %multiply_convert_fusion.2) | copy-start | bytes 6291460
  88.7 7.0 %copy-start.11 = (f32[4,16,16,1024]{3,2,1,0:T(8,128)S(1)}, f32[4,16,16,1024]{3,2,1,0:T(8,128)}, u32[]{:S(2)}) copy-start(f32[4,16,16,1024]{3,2,1,0:T(8,128)} %copy.73) | copy-start | bytes 12582916
  88.7 7.0 %copy-start.12 = (f32[4,16,16,1024]{3,2,1,0:T(8,128)S(1)}, f32[4,16,16,1024]{3,2,1,0:T(8,128)}, u32[]{:S(2)}) copy-start(f32[4,16,16,1024]{3,2,1,0:T(8,128)} %copy.63) | copy-start | bytes 12582916
  88.7 7.1 %copy-start.21 = (f32[1,2,4,128]{3,1,2,0:T(2,128)S(1)}, f32[1,2,4,128]{3,1,2,0:T(2,128)}, u32[]{:S(2)}) copy-start(f32[1,2,4,128]{3,1,2,0:T(2,128)} %copy.82) | copy-start | bytes 12292
  88.7 9.4 %copy-start.22 = (bf16[2048,1024]{1,0:T(8,128)(2,1)S(1)}, bf16[2048,1024]{1,0:T(8,128)(2,1)}, u32[]{:S(2)}) copy-start(bf16[2048,1024]{1,0:T(8,128)(2,1)} %param.13) | copy-start | bytes 12582916
  88.8 9.4 %copy-start.24 = (f32[1024]{0:T(1024)S(1)}, f32[1024]{0:T(1024)}, u32[]{:S(2)}) copy-start(f32[1024]{0:T(1024)} %param.14) | copy-start | bytes 12292
  95.8 9.2 %copy-start.27 = (bf16[1024,2048]{1,0:T(8,128)(2,1)}, bf16[1024,2048]{1,0:T(8,128)(2,1)S(1)}, u32[]{:S(2)}) copy-start(bf16[1024,2048]{1,0:T(8,128)(2,1)S(1)} %get-tuple-element.116) | copy-start | bytes 12582916
  105.0 9.9 %copy-start.28 = (bf16[1024,1024]{1,0:T(8,128)(2,1)}, bf16[1024,1024]{1,0:T(8,128)(2,1)S(1)}, u32[]{:S(2)}) copy-start(bf16[1024,1024]{1,0:T(8,128)(2,1)S(1)} %get-tuple-element.96) | copy-start | bytes 6291460
  105.0 9.9 %copy-start.2 = (f32[4,16,16,1024]{3,2,1,0:T(8,128)S(1)}, f32[4,16,16,1024]{3,2,1,0:T(8,128)}, u32[]{:S(2)}) copy-start(f32[4,16,16,1024]{3,2,1,0:T(8,128)} %copy.68) | copy-start | bytes 12582916
  114.9 5.1 copy-start.26
  122.5 8.2 %copy-start.1 = (bf16[4,22,16,1024]{3,0,2,1:T(4,128)(2,1)S(1)}, bf16[4,22,16,1024]{3,0,2,1:T(4,128)(2,1)}, u32[]{:S(2)}) copy-start(bf16[4,22,16,1024]{3,0,2,1:T(4,128)(2,1)} %copy-done) | copy-start | bytes 8650756
  172.0 10.9 %copy-start.10 = (bf16[4,16,16,1024]{3,2,1,0:T(8,128)(2,1)S(1)}, bf16[4,16,16,1024]{3,2,1,0:T(8,128)(2,1)}, u32[]{:S(2)}) copy-start(bf16[4,16,16,1024]{3,2,1,0:T(8,128)(2,1)} %param.8) | copy-start | bytes 6291460
  210.0 279.1 %reduce-scatter.5.cloned.1.call-start = ((), (), s32[]{:S(2)}) async-start(), calls=%async_computation.3 | async-start | bytes 8650752 | tf_op jit(solution)/shard_map/reduce_scatter | solution.py:103
  220.7 415.8 %reduce-scatter.3.cloned.1.call-start = ((), (), s32[]{:S(2)}) async-start(), calls=%async_computation.2 | async-start | bytes 8650752 | tf_op jit(solution)/shard_map/reduce_scatter | solution.py:102
  232.0 13.0 %collective-permute-start.4 = (bf16[4,3,16,1024]{3,0,2,1:T(4,128)(2,1)S(1)}, bf16[4,3,16,1024]{3,0,2,1:T(4,128)(2,1)S(1)}, u32[]{:S(2)}, u32[]{:S(2)}) collective-permute-start(bf16[4,3,16,1024]{3,0,2,1:T(4,128)(2,1)S(1)} %copy.145), channel_id=1, source_target_pairs={{0,4},{4,8},{8,12},{1,5},{5,9},{9,13},{2,6},{6,10},{10,14},{3,7},{... | collective-permute-start | bytes 1179656 | tf_op jit(solution)/shard_map/ppermute | solution.py:20
  236.7 13.1 %collective-permute-start.5 = (bf16[4,3,16,1024]{3,0,2,1:T(4,128)(2,1)S(1)}, bf16[4,3,16,1024]{3,0,2,1:T(4,128)(2,1)S(1)}, u32[]{:S(2)}, u32[]{:S(2)}) collective-permute-start(bf16[4,3,16,1024]{3,0,2,1:T(4,128)(2,1)S(1)} %copy.146), channel_id=1, source_target_pairs={{4,0},{8,4},{12,8},{5,1},{9,5},{13,9},{6,2},{10,6},{14,10},{7,3},{... | collective-permute-start | bytes 1179656 | tf_op jit(solution)/shard_map/ppermute | solution.py:23
  245.1 11.6 %copy-start.18 = (bf16[49,1024]{1,0:T(8,128)(2,1)S(1)}, bf16[49,1024]{1,0:T(8,128)(2,1)}, u32[]{:S(2)}) copy-start(bf16[49,1024]{1,0:T(8,128)(2,1)} %param.10) | copy-start | bytes 301060
  247.0 92.3 %copy-start.14 = (bf16[4,16,16,1024]{3,2,1,0:T(8,128)(2,1)S(1)}, bf16[4,16,16,1024]{3,2,1,0:T(8,128)(2,1)}, u32[]{:S(2)}) copy-start(bf16[4,16,16,1024]{3,2,1,0:T(8,128)(2,1)} %param.15) | copy-start | bytes 6291460
  252.0 87.3 %collective-permute-start.6 = (bf16[4,22,3,1024]{3,0,2,1:T(4,128)(2,1)S(1)}, bf16[4,22,3,1024]{3,0,2,1:T(4,128)(2,1)}, u32[]{:S(2)}, u32[]{:S(2)}) collective-permute-start(bf16[4,22,3,1024]{3,0,2,1:T(4,128)(2,1)S(1)} %get-tuple-element.98), channel_id=1, source_target_pairs={{0,1},{1,2},{2,3},{4,5},{5,6},{6,7},{8,9},{9,10},{10,11},{12,13},{... | collective-permute-start | bytes 1622024 | tf_op jit(solution)/shard_map/ppermute | solution.py:20
  255.4 83.9 %collective-permute-start.7 = (bf16[4,22,3,1024]{3,0,2,1:T(4,128)(2,1)S(1)}, bf16[4,22,3,1024]{3,0,2,1:T(4,128)(2,1)}, u32[]{:S(2)}, u32[]{:S(2)}) collective-permute-start(bf16[4,22,3,1024]{3,0,2,1:T(4,128)(2,1)S(1)} %get-tuple-element.99), channel_id=1, source_target_pairs={{1,0},{2,1},{3,2},{5,4},{6,5},{7,6},{9,8},{10,9},{11,10},{13,12},{... | collective-permute-start | bytes 1622024 | tf_op jit(solution)/shard_map/ppermute | solution.py:23
  (8 other events, 19.1 us)
Sparse Core Ops, SparseCore 0:
  210.1 127.5 all-reduce.2
  340.0 149.0 reduce-scatter.4
  491.4 145.0 reduce-scatter.2
where the time goes:
time: 654 us; the launch traced here: 645 us
  waiting for transfers between devices  323 us (49%)
  other arithmetic  103 us (16%)
  matrix products  99.9 us (15%)
  blocking collectives  43 us (7%)
  local copies, waits for them, and re-layouts  41.5 us (6%)
  starting transfers between devices  20.5 us (3%)
  between operations  14.7 us (2%)
    reduce_scatter x1, waiting for transfers between devices, shards(): lax.psum_scatter(w_in_term, ('dp', 'row', 'col'), scatter_dimension=0, ti...  146 us
    reduce_scatter x1, waiting for transfers between devices, shards(): lax.psum_scatter(w_out_term, ('dp', 'row', 'col'), scatter_dimension=0, t...  124 us
    reduce_sum x8, other arithmetic, shards(): dw_terms.append(jnp.sum(g_wide * window, axis=(0, 1, 2)))  82.7 us
    conv_general_dilated x2, matrix products, depthwise(): lax.conv_general_dilated(padded, taps, (1, 1), 'VALID', dimension_numbers...  49.8 us
    psum x1, blocking collectives, shards(): lax.psum((dw_term, gain_contribution, gamma_term), ('dp', 'row', 'col'))  43 us
    psum x1, waiting for transfers between devices, shards(): lax.psum((dw_term, gain_contribution, gamma_term), ('dp', 'row', 'col'))  37 us
    ppermute x4, starting transfers between devices, extended(): lax.ppermute(lax.slice_in_dim(block, block.shape[dim] - width, None, axis...  15 us
    ppermute x4, waiting for transfers between devices, extended(): lax.ppermute(lax.slice_in_dim(block, block.shape[dim] - width, None, axis...  13.7 us
  transfers between devices with their start and end apart: 11, of which 6 were waited for; matrix products, arithmetic and copies ran while one was open for 12% of the time, Pallas kernels for 0%

commit v1 on v0

--- a/solution.py
+++ b/solution.py
@@ -3,6 +3,8 @@
 import jax
 import jax.numpy as jnp
 from jax import lax
+from jax.experimental import pallas as pl
+from jax.experimental.pallas import tpu as pltpu
 from jax.sharding import PartitionSpec as P
 
 KERNEL = 7
@@ -25,17 +27,135 @@
     return block
 
 
-def depthwise(padded, kernel, width):
-    taps = kernel.reshape(KERNEL, KERNEL, 1, width)
-    return lax.conv_general_dilated(
-        padded,
-        taps,
-        (1, 1),
-        "VALID",
-        dimension_numbers=("NHWC", "HWIO", "NHWC"),
-        feature_group_count=width,
-        preferred_element_type=jnp.float32,
-    )
+LANES = 128
+
+
+def shifted_views(source, views, tile_w):
+    wide = source[0].astype(jnp.float32)
+    for j in range(KERNEL):
+        views[j] = wide[:, j : j + tile_w, :]
+
+
+def conv_kernel(x_ref, w_ref, *rest):
+    extra, o_ref, views = (rest[0] if len(rest) == 3 else None), rest[-2], rest[-1]
+    tile_h, tile_w = o_ref.shape[1], o_ref.shape[2]
+    shifted_views(x_ref, views, tile_w)
+    half = tile_h // 2
+    for top in range(0, tile_h, half):
+        acc = jnp.zeros((half, tile_w, LANES), jnp.float32)
+        for i in range(KERNEL):
+            for j in range(KERNEL):
+                tap = i * KERNEL + j
+                weight = w_ref[tap : tap + 1, :][None]
+                acc = acc + views[j, top + i : top + i + half] * weight
+        if extra is not None:
+            acc = acc + extra[0, top : top + half].astype(jnp.float32)
+        o_ref[0, top : top + half] = acc.astype(o_ref.dtype)
+
+
+def depthwise(padded, weights, extra, dtype):
+    batch, full_h, full_w, width = padded.shape
+    tile_h, tile_w = full_h - KERNEL + 1, full_w - KERNEL + 1
+    cell_spec = pl.BlockSpec((1, tile_h, tile_w, LANES), lambda c, n: (n, 0, 0, c))
+    in_specs = [
+        pl.BlockSpec((1, full_h, full_w, LANES), lambda c, n: (n, 0, 0, c)),
+        pl.BlockSpec((KERNEL * KERNEL, LANES), lambda c, n: (0, c)),
+    ]
+    operands = [padded, weights.astype(jnp.float32)]
+    if extra is not None:
+        in_specs.append(cell_spec)
+        operands.append(extra)
+    size = batch * tile_h * tile_w * width
+    return pl.pallas_call(
+        conv_kernel,
+        grid=(width // LANES, batch),
+        in_specs=in_specs,
+        out_specs=cell_spec,
+        out_shape=jax.ShapeDtypeStruct((batch, tile_h, tile_w, width), dtype),
+        scratch_shapes=[pltpu.VMEM((KERNEL, full_h, tile_w, LANES), jnp.float32)],
+        compiler_params=pltpu.CompilerParams(vmem_limit_bytes=24 * 2**20),
+        cost_estimate=pl.CostEstimate(flops=98 * size * 150, bytes_accessed=6 * size, transcendentals=0),
+    )(*operands)
+
+
+def dw_kernel(x_ref, g_ref, o_ref, views, total):
+    step = pl.program_id(1)
+    tile_h, tile_w = g_ref.shape[1], g_ref.shape[2]
+    shifted_views(x_ref, views, tile_w)
+
+    @pl.when(step == 0)
+    def _():
+        total[...] = jnp.zeros_like(total)
+
+    half = tile_h // 2
+    for top in range(0, tile_h, half):
+        g = g_ref[0, top : top + half].astype(jnp.float32)
+        for i in range(KERNEL):
+            for j in range(KERNEL):
+                part = jnp.sum(views[j, top + i : top + i + half] * g, axis=0)
+                part = jnp.sum(part.reshape(tile_w // 8, 8, LANES), axis=0)
+                total[i * KERNEL + j] += part
+
+    @pl.when(step == pl.num_programs(1) - 1)
+    def _():
+        o_ref[...] = jnp.sum(total[...], axis=1)
+
+
+def kernel_gradient(padded, g_conv):
+    batch, full_h, full_w, width = padded.shape
+    tile_h, tile_w = full_h - KERNEL + 1, full_w - KERNEL + 1
+    size = batch * tile_h * tile_w * width
+    return pl.pallas_call(
+        dw_kernel,
+        grid=(width // LANES, batch),
+        in_specs=[
+            pl.BlockSpec((1, full_h, full_w, LANES), lambda c, n: (n, 0, 0, c)),
+            pl.BlockSpec((1, tile_h, tile_w, LANES), lambda c, n: (n, 0, 0, c)),
+        ],
+        out_specs=pl.BlockSpec((KERNEL * KERNEL, LANES), lambda c, n: (0, c)),
+        out_shape=jax.ShapeDtypeStruct((KERNEL * KERNEL, width), jnp.float32),
+        scratch_shapes=[
+            pltpu.VMEM((KERNEL, full_h, tile_w, LANES), jnp.float32),
+            pltpu.VMEM((KERNEL * KERNEL, 8, LANES), jnp.float32),
+        ],
+        compiler_params=pltpu.CompilerParams(vmem_limit_bytes=24 * 2**20),
+        cost_estimate=pl.CostEstimate(flops=98 * size * 150, bytes_accessed=6 * size, transcendentals=0),
+    )(padded, g_conv)
+
+
+def halved(term, order):
+    names = ("dp", "row", "col")
+    sizes = [lax.axis_size(name) for name in names]
+    devices = math.prod(sizes)
+    rows = term.shape[0] // devices
+    part = term.reshape(*sizes, rows, term.shape[1])
+    done = {name: 0 for name in names}
+    for name in order:
+        dim, count = names.index(name), lax.axis_size(name)
+        stride = 2 ** done[name]
+        done[name] += 1
+        index = lax.axis_index(name)
+        bit = (index // stride) % 2
+        left = part.shape[dim]
+        shape = part.shape[:dim] + (left // 2, 2) + part.shape[dim + 1 :]
+        pairs = part.reshape(shape)
+        mine = lax.dynamic_index_in_dim(pairs, bit, dim + 1, keepdims=False)
+        theirs = lax.dynamic_index_in_dim(pairs, 1 - bit, dim + 1, keepdims=False)
+        swap = [(k, k ^ stride) for k in range(count)]
+        got = lax.ppermute(theirs.astype(jnp.bfloat16), name, swap)
+        part = mine.astype(jnp.float32) + got.astype(jnp.float32)
+        if sum(done.values()) < len(order):
+            part = part.astype(jnp.bfloat16)
+    return part.reshape(rows, term.shape[1])
+
+
+def steps_of(*names):
+    bits = {name: int(math.log2(lax.axis_size(name))) for name in names}
+    bits["col"] -= 1
+    order = ["col"]
+    for name in names:
+        order += [name] * bits[name]
+    return order
 
 
 def extend(field):
@@ -47,7 +167,7 @@
     cells = tile_h * tile_w
     total_rows = batch * cells
     padded = extend(images_in)
-    conv = depthwise(padded, dw_weight, width).reshape(total_rows, width)
+    conv = depthwise(padded, dw_weight, None, jnp.float32).reshape(total_rows, width)
     mean_v = jnp.mean(conv, axis=-1, keepdims=True)
     local_device = conv - mean_v
     inverse_deviation = lax.rsqrt(
@@ -82,34 +202,26 @@
         )
     ).astype(jnp.bfloat16)
     g_conv4 = convolution_gradient.reshape(batch, tile_h, tile_w, width)
-    g_wide = g_conv4.astype(jnp.float32)
-    dw_terms = []
-    for i in range(KERNEL):
-        for j in range(KERNEL):
-            window = padded[:, i : i + tile_h, j : j + tile_w, :].astype(jnp.float32)
-            dw_terms.append(jnp.sum(g_wide * window, axis=(0, 1, 2)))
-    dw_term = jnp.stack(dw_terms, axis=0)
+    dw_term = kernel_gradient(padded, g_conv4)
     flipped = dw_weight.reshape(KERNEL, KERNEL, width)[::-1, ::-1].reshape(KERNEL * KERNEL, width)
-    back = depthwise(extend(g_conv4), flipped, width).reshape(total_rows, width)
-    grad_input = (upstream + back).astype(jnp.bfloat16).reshape(images_in.shape)
+    grad_input = depthwise(extend(g_conv4), flipped, out_grad, jnp.bfloat16)
     images = jnp.float32(batch * lax.axis_size("dp"))
-    dw_sum, gain_sum, gamma_sum = lax.psum(
-        (dw_term, gain_contribution, gamma_term), ("dp", "row", "col")
-    )
-    w_in_term = jnp.dot(normalized_input.T, g_pre, preferred_element_type=jnp.float32)
-    w_out_term = jnp.dot(hidden.T, g_branch, preferred_element_type=jnp.float32)
-    w_in_sum, w_out_sum = (
-        lax.psum_scatter(w_in_term, ("dp", "row", "col"), scatter_dimension=0, tiled=True),
-        lax.psum_scatter(w_out_term, ("dp", "row", "col"), scatter_dimension=0, tiled=True),
-    )
+    small = jnp.concatenate([dw_term, gain_contribution[None], gamma_term[None]], axis=0)
+    small = lax.psum(small, ("dp", "row", "col")) / images
+    taps = KERNEL * KERNEL
+    dw_sum, gain_sum, gamma_sum = small[:taps], small[taps], small[taps + 1]
+    w_out_term = jnp.dot(hidden.T, g_branch, preferred_element_type=jnp.float32).astype(jnp.bfloat16)
+    w_in_term = jnp.dot(normalized_input.T, g_pre, preferred_element_type=jnp.float32).astype(jnp.bfloat16)
+    w_out_sum = halved(w_out_term, steps_of("col", "row", "dp"))
+    w_in_sum = halved(w_in_term, steps_of("dp", "row", "col"))
     return (
         output,
         grad_input,
         w_in_sum / images,
         w_out_sum / images,
-        dw_sum / images,
-        gain_sum / images,
-        gamma_sum / images,
+        dw_sum,
+        gain_sum,
+        gamma_sum,
     )
 
 

time: 654 us -> 377 us (0.58); the launches traced: 645 us -> 377 us
  waiting for transfers between devices: 323 us -> 175 us
  other arithmetic: 103 us -> 25.9 us
  matrix products: 99.9 us -> 37.9 us
  Pallas kernels: 0 us -> 59.9 us
  blocking collectives: 43 us -> 0 us
  starting transfers between devices: 20.5 us -> 40 us
  local copies, waits for them, and re-layouts: 41.5 us -> 23.5 us
    reduce_scatter x2 -> x0, waiting for transfers between devices: 269 us -> none  [the longest x1 146 us: shards(): lax.psum_scatter(w_in_term, ('dp', 'row', 'col'), scatter_dimension=0, ti...]
    psum x1, waiting for transfers between devices: 37 us -> 123 us  [shards(): small = lax.psum(small, ('dp', 'row', 'col')) / images]
    reduce_sum x8 -> x1, other arithmetic: 82.7 us -> 2.46 us  [shards(): mean_v = jnp.mean(conv, axis=-1, keepdims=True)]
    pallas_call x0 -> x3, Pallas kernels: none -> 59.9 us  [the longest x2 39.3 us: depthwise(): pl.pallas_call(conv_kernel, grid=(width // LANES, batch), in_specs=in_spe...]
    conv_general_dilated x2 -> x0, matrix products: 49.8 us -> none  [depthwise(): lax.conv_general_dilated(padded, taps, (1, 1), 'VALID', dimension_numbers...]
    psum x1 -> x0, blocking collectives: 43 us -> none  [shards(): lax.psum((dw_term, gain_contribution, gamma_term), ('dp', 'row', 'col'))]
    ppermute x0 -> x10, waiting for transfers between devices: none -> 40.5 us  [halved(): got = lax.ppermute(theirs.astype(jnp.bfloat16), name, swap)]
    ppermute x0 -> x10, starting transfers between devices: none -> 21 us  [halved(): got = lax.ppermute(theirs.astype(jnp.bfloat16), name, swap)]
  transfers between devices with their start and end apart: 11 -> 19, of which waited for: 6 -> 8; matrix products, arithmetic and copies ran while one was open for 12% -> 7% of each run, Pallas kernels for 0% -> 11%
where the time goes in v1:
time: 377 us
  waiting for transfers between devices  175 us (46%)
  Pallas kernels  59.9 us (16%)
  starting transfers between devices  40 us (11%)
  matrix products  37.9 us (10%)
  other arithmetic  25.9 us (7%)
  local copies, waits for them, and re-layouts  23.5 us (6%)
  between operations  14.8 us (4%)
    psum x1, waiting for transfers between devices, shards(): small = lax.psum(small, ('dp', 'row', 'col')) / images  123 us
    ppermute x10, waiting for transfers between devices, halved(): got = lax.ppermute(theirs.astype(jnp.bfloat16), name, swap)  40.5 us
    pallas_call x2, Pallas kernels, depthwise(): pl.pallas_call(conv_kernel, grid=(width // LANES, batch), in_specs=in_spe...  39.3 us
    ppermute x10, starting transfers between devices, halved(): got = lax.ppermute(theirs.astype(jnp.bfloat16), name, swap)  21 us
    pallas_call x1, Pallas kernels, kernel_gradient(): pl.pallas_call(dw_kernel, grid=(width // LANES, batch), in_specs=[pl.Bloc...  20.6 us
    ppermute x4, starting transfers between devices, extended(): lax.ppermute(lax.slice_in_dim(block, block.shape[dim] - width, None, axis...  13.4 us
    dot_general x1, matrix products, shards(): jnp.dot(g_branch, w_out.T, preferred_element_type=jnp.float32) * slope  9.22 us
  transfers between devices with their start and end apart: 19, of which 8 were waited for; matrix products, arithmetic and copies ran while one was open for 7% of the time, Pallas kernels for 11%

profile of v1, /device:TPU:0, one launch (start us, length us, event | category | flops | bytes accessed | tf_op | source)
XLA Modules:
  0.0 376.9 jit_solution(1161234273631113976)
XLA Ops:
  8.4 5.0 %collective-permute-start = (bf16[4,3,16,1024]{3,2,1,0:T(8,128)(2,1)S(1)}, bf16[4,3,16,1024]{3,2,1,0:T(8,128)(2,1)S(1)}, u32[]{:S(2)}, u32[]{:S(2)}) collective-permute-start(bf16[4,3,16,1024]{3,2,1,0:T(8,128)(2,1)S(1)} %get-tuple-element.22), channel_id=1, source_target_pairs={{0,4},{4,8},{8,12},{1,5},{5,9},{9,13},{2,6},{6,10},{10,14},{3,7},{... | collective-permute-start | bytes 1179656 | tf_op jit(solution)/shard_map/ppermute | solution.py:22
  14.7 7.0 %collective-permute-done = bf16[4,3,16,1024]{3,2,1,0:T(8,128)(2,1)S(1)} collective-permute-done((bf16[4,3,16,1024]{3,2,1,0:T(8,128)(2,1)S(1)}, bf16[4,3,16,1024]{3,2,1,0:T(8,128)(2,1)S(1)}, u32[]{:S(2)}, u32[]{:S(2)}) %collective-permute-start) | collective-permute-done | bytes 393248 | tf_op jit(solution)/shard_map/ppermute | solution.py:22
  23.7 2.1 collective-permute-done.1
  27.8 2.1 collective-permute-start.2
  37.7 2.7 pad_maximum_fusion.x_ref
  40.4 19.0 %shard_map.135 = f32[4,16,16,1024]{3,2,1,0:T(8,128)S(1)} custom-call(bf16[4,22,22,1024]{3,2,1,0:T(8,128)(2,1)S(1)} %pad_maximum_fusion.x_ref, f32[49,1024]{1,0:T(8,128)S(1)} %convert_element_type.174.w_ref), custom_call_target="tpu_custom_call" | custom-call | flops 15414067200 | bytes 6291456 | tf_op jit(solution)/shard_map/pallas_call | solution.py:69
  63.3 2.5 reduce_sum.54
  65.8 2.7 multiply_reduce_fusion.2
  68.7 2.9 multiply_convert_fusion.2
  72.2 7.0 %multiply_convert_fusion = (bf16[1024,2048]{1,0:T(8,128)(2,1)S(1)}, f32[1024,2048]{1,0:T(8,128)}) fusion(bf16[1024,1024]{1,0:T(8,128)(2,1)S(1)} %multiply_convert_fusion.2, bf16[1024,2048]{1,0:T(8,128)(2,1)S(1)} %copy-done.13), kind=kOutput, calls=%fused_computation.7 | convolution fusion | flops 4305453056 | bytes 18874368 | tf_op jit(solution)/shard_map/dot_general | solution.py:178
  79.2 6.7 %fusion.7 = (f32[1024]{0:T(1024)S(1)}, bf16[1024,1024]{1,0:T(8,128)(2,1)}, bf16[1024,1024]{1,0:T(8,128)(2,1)S(1)}) fusion(bf16[4,16,16,1024]{3,2,1,0:T(8,128)(2,1)S(1)} %copy-done.3, f32[1024]{0:T(1024)S(1)} %bitcast.90, f32[1024]{0:T(1024)S(1)} %copy-done.14, bf16[4,16,16,1024]{3,2,1,0:T(8,128)(2,1)S(1)} %copy-done.8, ...), kind=kOutput, calls=%fused_computation.15 | convolution fusion | flops 4306500608 | bytes 16789504 | tf_op jit(solution)/shard_map/dot_general | solution.py:181
  86.0 4.9 %convolution_convert_fusion = bf16[2048,1024]{1,0:T(8,128)(2,1)S(1)} fusion(bf16[1024,2048]{1,0:T(8,128)(2,1)S(1)} %get-tuple-element.25, bf16[1024,1024]{1,0:T(8,128)(2,1)S(1)} %get-tuple-element.18), kind=kOutput, calls=%fused_computation.30 | convolution fusion | flops 4297064448 | bytes 10485760 | tf_op jit(solution)/shard_map/dot_general | solution.py:213
  90.9 9.2 %fusion.5 = bf16[1024,2048]{1,0:T(8,128)(2,1)S(1)} fusion(f32[1024,2048]{1,0:T(8,128)} %get-tuple-element.26, bf16[1024,1024]{1,0:T(8,128)(2,1)S(1)} %get-tuple-element.18, bf16[2048,1024]{1,0:T(8,128)(2,1)S(1)} %copy-done.12), kind=kOutput, calls=%fused_computation.6 | convolution fusion | flops 4315938816 | bytes 18874368 | tf_op jit(solution)/shard_map/dot_general | solution.py:189
  100.1 5.1 %multiply_reduce_fusion = (f32[1024]{0:T(1024)S(1)}, f32[1024]{0:T(1024)S(1)}, f32[1024]{0:T(1024)S(1)}, f32[1024,1024]{1,0:T(8,128)S(1)}) fusion(f32[4,16,16,1024]{3,2,1,0:T(8,128)S(1)} %copy-done.1, f32[1024]{0:T(1024)S(1)} %rsqrt.12, f32[1024]{0:T(1024)S(1)} %div.64, f32[1024]{0:T(1024)S(1)} %copy-done.11, bf16[1024,2048]{1,0:T(8,128)(2,1)S(1)} %fusion.5, ...), kind=kOutput, calls=%fused_computation.25 | convolution fusion | flops 4303352832 | bytes 16801792 | tf_op jit(solution)/shard_map/dot_general | solution.py:192
  105.2 4.9 %convolution_convert_fusion.1 = bf16[1024,2048]{1,0:T(8,128)(2,1)S(1)} fusion(bf16[1024,1024]{1,0:T(8,128)(2,1)S(1)} %multiply_convert_fusion.2, bf16[1024,2048]{1,0:T(8,128)(2,1)S(1)} %fusion.5), kind=kOutput, calls=%fused_computation.31 | convolution fusion | flops 4297064448 | bytes 10485760 | tf_op jit(solution)/shard_map/dot_general | solution.py:214
  110.2 2.2 constant_dynamic-slice_fusion.4
  113.9 7.3 %collective-permute-start.13 = (bf16[2,4,2,64,1024]{4,3,1,0,2:T(8,128)(2,1)}, bf16[2,4,2,64,1024]{4,3,1,0,2:T(8,128)(2,1)}, u32[]{:S(2)}, u32[]{:S(2)}) collective-permute-start(bf16[2,4,2,64,1024]{4,3,1,0,2:T(8,128)(2,1)} %bitcast.72), channel_id=1, source_target_pairs={{0,1},{1,0},{2,3},{3,2},{4,5},{5,4},{6,7},{7,6},{8,9},{9,8},{10,11... | collective-permute-start | bytes 6291464 | tf_op jit(solution)/shard_map/ppermute | solution.py:145
  125.5 3.5 collective-permute-start.4
  130.3 20.6 %shard_map.137 = f32[49,1024]{1,0:T(8,128)S(1)} custom-call(bf16[4,22,22,1024]{3,2,1,0:T(8,128)(2,1)S(1)} %bitcast.79, bf16[4,16,16,1024]{3,2,1,0:T(8,128)(2,1)S(1)} %bitcast.75), custom_call_target="tpu_custom_call" | custom-call | flops 15414067200 | bytes 6291456 | tf_op jit(solution)/shard_map/pallas_call | solution.py:108
  152.3 123.1 %all-reduce.2.cloned.1.call-done = f32[51,1024]{1,0:T(8,128)} async-done(((f32[51,1024]{1,0:T(8,128)}), f32[51,1024]{1,0:T(8,128)}) %all-reduce.2.cloned.1.call-update) | async-done | bytes 208912 | tf_op jit(solution)/shard_map/psum | solution.py:210
  277.7 2.8 collective-permute-start.6
  282.7 2.7 fusion.11
  285.5 3.0 collective-permute-start.14
  288.5 2.5 fusion.12
  293.3 2.9 pad_maximum_fusion.1.x_ref
  296.3 18.8 %collective-permute-done.14 = bf16[2,4,1,64,1024]{4,3,1,0,2:T(8,128)(2,1)S(1)} collective-permute-done((bf16[2,4,1,64,1024]{4,3,1,0,2:T(8,128)(2,1)S(1)}, bf16[2,4,1,64,1024]{4,3,1,0,2:T(8,128)(2,1)S(1)}, u32[]{:S(2)}, u32[]{:S(2)}) %collective-permute-start.14) | collective-permute-done | bytes 1048608 | tf_op jit(solution)/shard_map/ppermute | solution.py:145
  315.6 3.3 collective-permute-start.15
  319.4 20.4 %shard_map.136 = bf16[4,16,16,1024]{3,2,1,0:T(8,128)(2,1)} custom-call(bf16[4,22,22,1024]{3,2,1,0:T(8,128)(2,1)S(1)} %pad_maximum_fusion.1.x_ref, f32[49,1024]{1,0:T(8,128)S(1)} %reshape.172.w_ref, bf16[4,16,16,1024]{3,2,1,0:T(8,128)(2,1)S(1)} %copy-done.4), custom_call_target="tpu_custom_call" | custom-call | flops 15414067200 | bytes 6291456 | tf_op jit(solution)/shard_map/pallas_call | solution.py:69
  343.3 15.2 %collective-permute-done.16 = bf16[2,1,1,64,1024]{4,3,1,0,2:T(8,128)(2,1)S(1)} collective-permute-done((bf16[2,1,1,64,1024]{4,3,1,0,2:T(8,128)(2,1)S(1)}, bf16[2,1,1,64,1024]{4,3,1,0,2:T(8,128)(2,1)S(1)}, u32[]{:S(2)}, u32[]{:S(2)}) %collective-permute-start.16) | collective-permute-done | bytes 262176 | tf_op jit(solution)/shard_map/ppermute | solution.py:145
  359.3 3.6 collective-permute-done.11
  362.9 2.7 collective-permute-start.12
  366.4 2.9 collective-permute-done.12
  (110 shorter events, 40.7 us)
Async XLA Ops:
  7.2 268.2 %all-reduce.2.cloned.1.call-start = ((), (), s32[]{:S(2)}) async-start(), calls=%async_computation | async-start | bytes 458752 | tf_op jit(solution)/shard_map/psum | solution.py:210
  8.4 13.3 %collective-permute-start = (bf16[4,3,16,1024]{3,2,1,0:T(8,128)(2,1)S(1)}, bf16[4,3,16,1024]{3,2,1,0:T(8,128)(2,1)S(1)}, u32[]{:S(2)}, u32[]{:S(2)}) collective-permute-start(bf16[4,3,16,1024]{3,2,1,0:T(8,128)(2,1)S(1)} %get-tuple-element.22), channel_id=1, source_target_pairs={{0,4},{4,8},{8,12},{1,5},{5,9},{9,13},{2,6},{6,10},{10,14},{3,7},{... | collective-permute-start | bytes 1179656 | tf_op jit(solution)/shard_map/ppermute | solution.py:22
  13.3 12.5 %collective-permute-start.1 = (bf16[4,3,16,1024]{3,2,1,0:T(8,128)(2,1)S(1)}, bf16[4,3,16,1024]{3,2,1,0:T(8,128)(2,1)S(1)}, u32[]{:S(2)}, u32[]{:S(2)}) collective-permute-start(bf16[4,3,16,1024]{3,2,1,0:T(8,128)(2,1)S(1)} %get-tuple-element.21), channel_id=1, source_target_pairs={{4,0},{8,4},{12,8},{5,1},{9,5},{13,9},{6,2},{10,6},{14,10},{7,3},{... | collective-permute-start | bytes 1179656 | tf_op jit(solution)/shard_map/ppermute | solution.py:25
  21.7 11.0 %copy-start.9 = (bf16[49,1024]{1,0:T(8,128)(2,1)S(1)}, bf16[49,1024]{1,0:T(8,128)(2,1)}, u32[]{:S(2)}) copy-start(bf16[49,1024]{1,0:T(8,128)(2,1)} %param.10) | copy-start | bytes 301060
  23.7 9.1 %copy-start.15 = (s32[4]{0:T(128)S(1)}, s32[4]{0:T(128)}, u32[]{:S(2)}) copy-start(s32[4]{0:T(128)} %param.9) | copy-start | bytes 52
  27.8 5.0 %collective-permute-start.2 = (bf16[4,22,3,1024]{3,0,2,1:T(4,128)(2,1)}, bf16[4,22,3,1024]{3,0,2,1:T(4,128)(2,1)}, u32[]{:S(2)}, u32[]{:S(2)}) collective-permute-start(bf16[4,22,3,1024]{3,0,2,1:T(4,128)(2,1)} %copy.18), channel_id=1, source_target_pairs={{0,1},{1,2},{2,3},{4,5},{5,6},{6,7},{8,9},{9,10},{10,11},{12,13},{... | collective-permute-start | bytes 1622024 | tf_op jit(solution)/shard_map/ppermute | solution.py:22
  31.2 5.1 %collective-permute-start.3 = (bf16[4,22,3,1024]{3,0,2,1:T(4,128)(2,1)}, bf16[4,22,3,1024]{3,0,2,1:T(4,128)(2,1)}, u32[]{:S(2)}, u32[]{:S(2)}) collective-permute-start(bf16[4,22,3,1024]{3,0,2,1:T(4,128)(2,1)} %copy.19), channel_id=1, source_target_pairs={{1,0},{2,1},{3,2},{5,4},{6,5},{7,6},{9,8},{10,9},{11,10},{13,12},{... | collective-permute-start | bytes 1622024 | tf_op jit(solution)/shard_map/ppermute | solution.py:25
  72.2 7.0 %copy-start.3 = (bf16[4,16,16,1024]{3,2,1,0:T(8,128)(2,1)S(1)}, bf16[4,16,16,1024]{3,2,1,0:T(8,128)(2,1)}, u32[]{:S(2)}) copy-start(bf16[4,16,16,1024]{3,2,1,0:T(8,128)(2,1)} %rest_0_.1) | copy-start | bytes 6291460
  72.2 7.0 %copy-start.8 = (bf16[4,16,16,1024]{3,2,1,0:T(8,128)(2,1)S(1)}, bf16[4,16,16,1024]{3,2,1,0:T(8,128)(2,1)}, u32[]{:S(2)}) copy-start(bf16[4,16,16,1024]{3,2,1,0:T(8,128)(2,1)} %param.8) | copy-start | bytes 6291460
  72.2 7.0 %copy-start.12 = (bf16[2048,1024]{1,0:T(8,128)(2,1)S(1)}, bf16[2048,1024]{1,0:T(8,128)(2,1)}, u32[]{:S(2)}) copy-start(bf16[2048,1024]{1,0:T(8,128)(2,1)} %param.13) | copy-start | bytes 12582916
  72.2 7.0 %copy-start.14 = (f32[1024]{0:T(1024)S(1)}, f32[1024]{0:T(1024)}, u32[]{:S(2)}) copy-start(f32[1024]{0:T(1024)} %param.14) | copy-start | bytes 12292
  90.9 9.2 %copy-start.1 = (f32[4,16,16,1024]{3,2,1,0:T(8,128)S(1)}, f32[4,16,16,1024]{3,2,1,0:T(8,128)}, u32[]{:S(2)}) copy-start(f32[4,16,16,1024]{3,2,1,0:T(8,128)} %copy-done) | copy-start | bytes 12582916
  110.2 11.1 %copy-start.6 = (bf16[1024,2048]{1,0:T(8,128)(2,1)}, bf16[1024,2048]{1,0:T(8,128)(2,1)S(1)}, u32[]{:S(2)}) copy-start(bf16[1024,2048]{1,0:T(8,128)(2,1)S(1)} %convolution_convert_fusion.1) | copy-start | bytes 12582916
  113.9 168.7 %collective-permute-start.13 = (bf16[2,4,2,64,1024]{4,3,1,0,2:T(8,128)(2,1)}, bf16[2,4,2,64,1024]{4,3,1,0,2:T(8,128)(2,1)}, u32[]{:S(2)}, u32[]{:S(2)}) collective-permute-start(bf16[2,4,2,64,1024]{4,3,1,0,2:T(8,128)(2,1)} %bitcast.72), channel_id=1, source_target_pairs={{0,1},{1,0},{2,3},{3,2},{4,5},{5,4},{6,7},{7,6},{8,9},{9,8},{10,11... | collective-permute-start | bytes 6291464 | tf_op jit(solution)/shard_map/ppermute | solution.py:145
  121.3 9.0 %slice-start = ((s8[4325376]{0:T(1024)(128)(4,1)}), s8[4194304]{0:T(1024)(128)(4,1)S(1)}, s32[]{:S(2)}) async-start(s8[4325376]{0:T(1024)(128)(4,1)} %bitcast.78), calls=%async_computation.1 | async-start | bytes 8388608
  122.8 165.6 %collective-permute-start.8 = (bf16[2,4,2,32,2048]{4,3,2,1,0:T(8,128)(2,1)}, bf16[2,4,2,32,2048]{4,3,2,1,0:T(8,128)(2,1)}, u32[]{:S(2)}, u32[]{:S(2)}) collective-permute-start(bf16[2,4,2,32,2048]{4,3,2,1,0:T(8,128)(2,1)} %dynamic-slice_bitcast_fusion), channel_id=1, source_target_pairs={{0,1},{1,0},{2,3},{3,2},{4,5},{5,4},{6,7},{7,6},{8,9},{9,8},{10,11... | collective-permute-start | bytes 6291464 | tf_op jit(solution)/shard_map/ppermute | solution.py:145
  122.8 7.5 %slice-start.1 = ((s8[4325376]{0:T(1024)(128)(4,1)}), s8[131072]{0:T(1024)(128)(4,1)S(1)}, s32[]{:S(2)}) async-start(s8[4325376]{0:T(1024)(128)(4,1)} %bitcast.78), calls=%async_computation.2 | async-start | bytes 262144
  125.5 151.0 %collective-permute-start.4 = (bf16[4,3,16,1024]{3,2,1,0:T(8,128)(2,1)}, bf16[4,3,16,1024]{3,2,1,0:T(8,128)(2,1)S(1)}, u32[]{:S(2)}, u32[]{:S(2)}) collective-permute-start(bf16[4,3,16,1024]{3,2,1,0:T(8,128)(2,1)} %get-tuple-element.19), channel_id=1, source_target_pairs={{0,4},{4,8},{8,12},{1,5},{5,9},{9,13},{2,6},{6,10},{10,14},{3,7},{... | collective-permute-start | bytes 1179656 | tf_op jit(solution)/shard_map/ppermute | solution.py:22
  129.0 147.5 %collective-permute-start.5 = (bf16[4,3,16,1024]{3,2,1,0:T(8,128)(2,1)}, bf16[4,3,16,1024]{3,2,1,0:T(8,128)(2,1)S(1)}, u32[]{:S(2)}, u32[]{:S(2)}) collective-permute-start(bf16[4,3,16,1024]{3,2,1,0:T(8,128)(2,1)} %get-tuple-element.20), channel_id=1, source_target_pairs={{4,0},{8,4},{12,8},{5,1},{9,5},{13,9},{6,2},{10,6},{14,10},{7,3},{... | collective-permute-start | bytes 1179656 | tf_op jit(solution)/shard_map/ppermute | solution.py:25
  275.3 7.3 %copy-start.5 = (bf16[2,4,2,1,64,1024]{5,4,3,2,1,0:T(8,128)(2,1)S(1)}, bf16[2,4,2,1,64,1024]{5,4,3,2,1,0:T(8,128)(2,1)}, u32[]{:S(2)}) copy-start(bf16[2,4,2,1,64,1024]{5,4,3,2,1,0:T(8,128)(2,1)} %get-tuple-element.12) | copy-start | bytes 6291460
  276.5 15.5 %copy-start.10 = (f32[51,1024]{1,0:T(8,128)}, f32[51,1024]{1,0:T(8,128)S(1)}, u32[]{:S(2)}) copy-start(f32[51,1024]{1,0:T(8,128)S(1)} %broadcast_multiply_fusion) | copy-start | bytes 626692
  277.7 14.8 %collective-permute-start.6 = (bf16[4,22,3,1024]{3,0,2,1:T(4,128)(2,1)S(1)}, bf16[4,22,3,1024]{3,0,2,1:T(4,128)(2,1)S(1)}, u32[]{:S(2)}, u32[]{:S(2)}) collective-permute-start(bf16[4,22,3,1024]{3,0,2,1:T(4,128)(2,1)S(1)} %copy.22), channel_id=1, source_target_pairs={{0,1},{1,2},{2,3},{4,5},{5,6},{6,7},{8,9},{9,10},{10,11},{12,13},{... | collective-permute-start | bytes 1622024 | tf_op jit(solution)/shard_map/ppermute | solution.py:22
  281.1 11.8 %collective-permute-start.7 = (bf16[4,22,3,1024]{3,0,2,1:T(4,128)(2,1)S(1)}, bf16[4,22,3,1024]{3,0,2,1:T(4,128)(2,1)S(1)}, u32[]{:S(2)}, u32[]{:S(2)}) collective-permute-start(bf16[4,22,3,1024]{3,0,2,1:T(4,128)(2,1)S(1)} %copy.23), channel_id=1, source_target_pairs={{1,0},{2,1},{3,2},{5,4},{6,5},{7,6},{9,8},{10,9},{11,10},{13,12},{... | collective-permute-start | bytes 1622024 | tf_op jit(solution)/shard_map/ppermute | solution.py:25
  285.5 29.6 %collective-permute-start.14 = (bf16[2,4,1,64,1024]{4,3,1,0,2:T(8,128)(2,1)S(1)}, bf16[2,4,1,64,1024]{4,3,1,0,2:T(8,128)(2,1)S(1)}, u32[]{:S(2)}, u32[]{:S(2)}) collective-permute-start(bf16[2,4,1,64,1024]{4,3,1,0,2:T(8,128)(2,1)S(1)} %constant_dynamic-slice_fusion.2), channel_id=1, source_target_pairs={{0,2},{1,3},{2,0},{3,1},{4,6},{5,7},{6,4},{7,5},{8,10},{9,11},{10,... | collective-permute-start | bytes 3145736 | tf_op jit(solution)/shard_map/ppermute | solution.py:145
  291.1 27.8 %collective-permute-start.9 = (bf16[1,4,2,32,2048]{4,3,2,1,0:T(8,128)(2,1)S(1)}, bf16[1,4,2,32,2048]{4,3,2,1,0:T(8,128)(2,1)S(1)}, u32[]{:S(2)}, u32[]{:S(2)}) collective-permute-start(bf16[1,4,2,32,2048]{4,3,2,1,0:T(8,128)(2,1)S(1)} %constant_dynamic-slice_fusion.7), channel_id=1, source_target_pairs={{0,16},{16,0},{1,17},{17,1},{2,18},{18,2},{3,19},{19,3},{4,20},{20... | collective-permute-start | bytes 3145736 | tf_op jit(solution)/shard_map/ppermute | solution.py:145
  296.2 23.2 %copy-start.4 = (bf16[4,16,16,1024]{3,2,1,0:T(8,128)(2,1)S(1)}, bf16[4,16,16,1024]{3,2,1,0:T(8,128)(2,1)}, u32[]{:S(2)}) copy-start(bf16[4,16,16,1024]{3,2,1,0:T(8,128)(2,1)} %rest_0_.1) | copy-start | bytes 6291460
  315.6 24.3 %collective-permute-start.15 = (bf16[2,2,1,64,1024]{4,3,1,0,2:T(8,128)(2,1)S(1)}, bf16[2,2,1,64,1024]{4,3,1,0,2:T(8,128)(2,1)S(1)}, u32[]{:S(2)}, u32[]{:S(2)}) collective-permute-start(bf16[2,2,1,64,1024]{4,3,1,0,2:T(8,128)(2,1)S(1)} %dynamic-slice_bitcast_fusion.1), channel_id=1, source_target_pairs={{0,4},{4,0},{8,12},{12,8},{1,5},{5,1},{9,13},{13,9},{2,6},{6,2},{1... | collective-permute-start | bytes 1572872 | tf_op jit(solution)/shard_map/ppermute | solution.py:145
  319.4 22.7 %collective-permute-start.10 = (bf16[1,2,2,32,2048]{4,3,2,1,0:T(8,128)(2,1)S(1)}, bf16[1,2,2,32,2048]{4,3,2,1,0:T(8,128)(2,1)S(1)}, u32[]{:S(2)}, u32[]{:S(2)}) collective-permute-start(bf16[1,2,2,32,2048]{4,3,2,1,0:T(8,128)(2,1)S(1)} %dynamic-slice_bitcast_fusion.2), channel_id=1, source_target_pairs={{0,4},{4,0},{8,12},{12,8},{1,5},{5,1},{9,13},{13,9},{2,6},{6,2},{1... | collective-permute-start | bytes 1572872 | tf_op jit(solution)/shard_map/ppermute | solution.py:145
  340.1 18.4 %collective-permute-start.16 = (bf16[2,1,1,64,1024]{4,3,1,0,2:T(8,128)(2,1)S(1)}, bf16[2,1,1,64,1024]{4,3,1,0,2:T(8,128)(2,1)S(1)}, u32[]{:S(2)}, u32[]{:S(2)}) collective-permute-start(bf16[2,1,1,64,1024]{4,3,1,0,2:T(8,128)(2,1)S(1)} %constant_dynamic-slice_fusion.1), channel_id=1, source_target_pairs={{0,8},{4,12},{8,0},{12,4},{1,9},{5,13},{9,1},{13,5},{2,10},{6,14},... | collective-permute-start | bytes 786440 | tf_op jit(solution)/shard_map/ppermute | solution.py:145
  342.3 20.6 %collective-permute-start.11 = (bf16[1,1,2,32,2048]{4,3,2,1,0:T(8,128)(2,1)S(1)}, bf16[1,1,2,32,2048]{4,3,2,1,0:T(8,128)(2,1)S(1)}, u32[]{:S(2)}, u32[]{:S(2)}) collective-permute-start(bf16[1,1,2,32,2048]{4,3,2,1,0:T(8,128)(2,1)S(1)} %constant_dynamic-slice_fusion.6), channel_id=1, source_target_pairs={{0,8},{4,12},{8,0},{12,4},{1,9},{5,13},{9,1},{13,5},{2,10},{6,14},... | collective-permute-start | bytes 786440 | tf_op jit(solution)/shard_map/ppermute | solution.py:145
  358.6 7.0 %collective-permute-start.17 = (bf16[1,1,1,64,1024]{4,3,1,0,2:T(8,128)(2,1)S(1)}, bf16[1,1,1,64,1024]{4,3,1,0,2:T(8,128)(2,1)S(1)}, u32[]{:S(2)}, u32[]{:S(2)}) collective-permute-start(bf16[1,1,1,64,1024]{4,3,1,0,2:T(8,128)(2,1)S(1)} %constant_dynamic-slice_fusion), channel_id=1, source_target_pairs={{0,16},{16,0},{1,17},{17,1},{2,18},{18,2},{3,19},{19,3},{4,20},{20... | collective-permute-start | bytes 393224 | tf_op jit(solution)/shard_map/ppermute | solution.py:145
  362.9 6.4 %collective-permute-start.12 = (bf16[1,1,1,32,2048]{4,3,2,1,0:T(8,128)(2,1)S(1)}, bf16[1,1,1,32,2048]{4,3,2,1,0:T(8,128)(2,1)S(1)}, u32[]{:S(2)}, u32[]{:S(2)}) collective-permute-start(bf16[1,1,1,32,2048]{4,3,2,1,0:T(8,128)(2,1)S(1)} %constant_dynamic-slice_fusion.5), channel_id=1, source_target_pairs={{0,2},{1,3},{2,0},{3,1},{4,6},{5,7},{6,4},{7,5},{8,10},{9,11},{10,... | collective-permute-start | bytes 393224 | tf_op jit(solution)/shard_map/ppermute | solution.py:145
  (5 other events, 18.6 us)
Sparse Core Ops, SparseCore 0:
  151.8 123.5 all-reduce.1

commit v2 on v1

v2 whole, which is shorter than its diff:
```python
import math

import jax
import jax.numpy as jnp
from jax import lax
from jax.experimental import pallas as pl
from jax.experimental.pallas import tpu as pltpu
from jax.sharding import PartitionSpec as P

KERNEL = 7


eps = 1e-06
keep_rate = 0.75


def extend(field, width=KERNEL // 2):
    rows, cols = lax.axis_size("row"), lax.axis_size("col")
    pieces = []
    for down in (-1, 0, 1):
        line = []
        for right in (-1, 0, 1):
            if down == 0 and right == 0:
                line.append(field)
                continue
            part = field
            for step, dim in ((down, 1), (right, 2)):
                full = field.shape[dim]
                if step == -1:
                    part = lax.slice_in_dim(part, full - width, None, axis=dim)
                elif step == 1:
                    part = lax.slice_in_dim(part, 0, width, axis=dim)
            pairs = []
            for r in range(rows):
                for c in range(cols):
                    if 0 <= r + down < rows and 0 <= c + right < cols:
                        pairs.append(((r + down) * cols + c + right, r * cols + c))
            line.append(lax.ppermute(part, ("row", "col"), pairs))
        pieces.append(line)
    return jnp.concatenate([jnp.concatenate(line, axis=2) for line in pieces], axis=1)


def extend_along(field, axis, dim, width=KERNEL // 2):
    forward = [(k, k + 1) for k in range(lax.axis_size(axis) - 1)]
    backward = [(target, source) for source, target in forward]
    full = field.shape[dim]
    low = lax.ppermute(lax.slice_in_dim(field, full - width, None, axis=dim), axis, forward)
    high = lax.ppermute(lax.slice_in_dim(field, 0, width, axis=dim), axis, backward)
    return jnp.concatenate([low, field, high], axis=dim)


def after(value, *others):
    return lax.optimization_barrier((value, *others))[0]


LANES = 128


def shifted_views(source, views, tile_w):
    wide = source[0].astype(jnp.float32)
    for j in range(KERNEL):
        views[j] = wide[:, j : j + tile_w, :]


def taps_sum(views, w_ref, top, rows, tile_w):
    acc = jnp.zeros((rows, tile_w, LANES), jnp.float32)
    for i in range(KERNEL):
        for j in range(KERNEL):
            tap = i * KERNEL + j
            acc = acc + views[j, top + i : top + i + rows] * w_ref[tap : tap + 1, :][None]
    return acc


def norm_kernel(x_ref, w_ref, gain_ref, xhat_ref, normed_ref, rstd_ref, views, held):
    step = pl.program_id(1)
    tile_h, tile_w, width = xhat_ref.shape[1:]
    shifted_views(x_ref, views, tile_w)
    half = tile_h // 2
    for top in range(0, tile_h, half):
        held[step, top : top + half] = taps_sum(views, w_ref, top, half, tile_w)

    @pl.when(step == pl.num_programs(1) - 1)
    def _():
        blocks = width // LANES

        @pl.loop(0, tile_h)
        def _(row):
            conv = [held[block, row] for block in range(blocks)]
            mean = jnp.sum(sum(conv), axis=-1, keepdims=True) / width
            centred = [part - mean for part in conv]
            spread = jnp.sum(sum(part * part for part in centred), axis=-1, keepdims=True)
            rstd = lax.rsqrt(spread / width + eps)
            rstd_ref[0, row] = rstd
            for block in range(blocks):
                lanes = slice(block * LANES, (block + 1) * LANES)
                xhat = centred[block] * rstd
                xhat_ref[0, row, :, lanes] = xhat
                normed_ref[0, row, :, lanes] = (xhat * gain_ref[:, lanes]).astype(jnp.bfloat16)


def conv_norm(padded, weights, gain):
    batch, full_h, full_w, width = padded.shape
    tile_h, tile_w = full_h - KERNEL + 1, full_w - KERNEL + 1
    size = batch * tile_h * tile_w * width
    shape = (batch, tile_h, tile_w, width)
    whole = pl.BlockSpec((1, tile_h, tile_w, width), lambda n, c: (n, 0, 0, 0))
    return pl.pallas_call(
        norm_kernel,
        grid=(batch, width // LANES),
        in_specs=[
            pl.BlockSpec((1, full_h, full_w, LANES), lambda n, c: (n, 0, 0, c)),
            pl.BlockSpec((KERNEL * KERNEL, LANES), lambda n, c: (0, c)),
            pl.BlockSpec((1, width), lambda n, c: (0, 0)),
        ],
        out_specs=[whole, whole, pl.BlockSpec((1, tile_h, tile_w, 1), lambda n, c: (n, 0, 0, 0))],
        out_shape=[
            jax.ShapeDtypeStruct(shape, jnp.float32),
            jax.ShapeDtypeStruct(shape, jnp.bfloat16),
            jax.ShapeDtypeStruct(shape[:3] + (1,), jnp.float32),
        ],
        scratch_shapes=[
            pltpu.VMEM((KERNEL, full_h, tile_w, LANES), jnp.float32),
            pltpu.VMEM((width // LANES, tile_h, tile_w, LANES), jnp.float32),
        ],
        compiler_params=pltpu.CompilerParams(vmem_limit_bytes=24 * 2**20),
        cost_estimate=pl.CostEstimate(flops=15000 * size, bytes_accessed=8 * size, transcendentals=0),
    )(padded, weights.astype(jnp.float32), gain[None])


def back_kernel(x_ref, w_ref, extra_ref, *rest):
    o_ref, views = rest[-2:]
    tile_h, tile_w = o_ref.shape[1], o_ref.shape[2]
    shifted_views(x_ref, views, tile_w)
    half = tile_h // 2
    for top in range(0, tile_h, half):
        acc = taps_sum(views, w_ref, top, half, tile_w)
        acc = acc + extra_ref[0, top : top + half].astype(jnp.float32)
        o_ref[0, top : top + half] = acc.astype(o_ref.dtype)


def conv_back(padded, weights, extra, start, count, earlier):
    batch, full_h, full_w, width = padded.shape
    tile_h, tile_w = full_h - KERNEL + 1, full_w - KERNEL + 1
    cell_spec = pl.BlockSpec((1, tile_h, tile_w, LANES), lambda c, n: (n + start, 0, 0, c))
    in_specs = [
        pl.BlockSpec((1, full_h, full_w, LANES), lambda c, n: (n + start, 0, 0, c)),
        pl.BlockSpec((KERNEL * KERNEL, LANES), lambda c, n: (0, c)),
        cell_spec,
    ]
    operands, aliases = [padded, weights.astype(jnp.float32), extra], {}
    if earlier is not None:
        in_specs.append(pl.BlockSpec(memory_space=pl.ANY))
        operands.append(earlier)
        aliases = {3: 0}
    size = count * tile_h * tile_w * width
    return pl.pallas_call(
        back_kernel,
        grid=(width // LANES, count),
        in_specs=in_specs,
        out_specs=cell_spec,
        out_shape=jax.ShapeDtypeStruct((batch, tile_h, tile_w, width), jnp.bfloat16),
        input_output_aliases=aliases,
        scratch_shapes=[pltpu.VMEM((KERNEL, full_h, tile_w, LANES), jnp.float32)],
        compiler_params=pltpu.CompilerParams(vmem_limit_bytes=24 * 2**20),
        cost_estimate=pl.CostEstimate(flops=15000 * size, bytes_accessed=6 * size, transcendentals=0),
    )(*operands)


def dw_kernel(x_ref, g_ref, o_ref, views, total):
    step = pl.program_id(1)
    tile_h, tile_w = g_ref.shape[1], g_ref.shape[2]
    shifted_views(x_ref, views, tile_w)

    @pl.when(step == 0)
    def _():
        total[...] = jnp.zeros_like(total)

    half = tile_h // 2
    for top in range(0, tile_h, half):
        g = g_ref[0, top : top + half].astype(jnp.float32)
        for i in range(KERNEL):
            for j in range(KERNEL):
                part = jnp.sum(views[j, top + i : top + i + half] * g, axis=0)
                part = jnp.sum(part.reshape(tile_w // 8, 8, LANES), axis=0)
                total[i * KERNEL + j] += part

    @pl.when(step == pl.num_programs(1) - 1)
    def _():
        o_ref[...] = jnp.sum(total[...], axis=1)


def kernel_gradient(padded, g_conv, part, parts):
    batch, full_h, full_w, width = padded.shape
    tile_h, tile_w = full_h - KERNEL + 1, full_w - KERNEL + 1
    blocks = width // LANES // parts
    start = blocks * part
    size = batch * tile_h * tile_w * blocks * LANES
    return pl.pallas_call(
        dw_kernel,
        grid=(blocks, batch),
        in_specs=[
            pl.BlockSpec((1, full_h, full_w, LANES), lambda c, n: (n, 0, 0, c + start)),
            pl.BlockSpec((1, tile_h, tile_w, LANES), lambda c, n: (n, 0, 0, c + start)),
        ],
        out_specs=pl.BlockSpec((KERNEL * KERNEL, LANES), lambda c, n: (0, c)),
        out_shape=jax.ShapeDtypeStruct((KERNEL * KERNEL, blocks * LANES), jnp.float32),
        scratch_shapes=[
            pltpu.VMEM((KERNEL, full_h, tile_w, LANES), jnp.float32),
            pltpu.VMEM((KERNEL * KERNEL, 8, LANES), jnp.float32),
        ],
        compiler_params=pltpu.CompilerParams(vmem_limit_bytes=24 * 2**20),
        cost_estimate=pl.CostEstimate(flops=15000 * size, bytes_accessed=6 * size, transcendentals=0),
    )(padded, g_conv)


class Halving:
    def __init__(self, term, order):
        names = ("dp", "row", "col")
        sizes = [lax.axis_size(name) for name in names]
        self.names, self.order = names, list(order)
        self.rows, self.columns = term.shape[0] // math.prod(sizes), term.shape[1]
        self.part = term.reshape(*sizes, self.rows, self.columns)
        self.done = {name: 0 for name in names}

    def step(self):
        name = self.order.pop(0)
        dim, count = self.names.index(name), lax.axis_size(name)
        stride = 2 ** self.done[name]
        self.done[name] += 1
        bit = (lax.axis_index(name) // stride) % 2
        part = self.part
        left = part.shape[dim]
        pairs = part.reshape(part.shape[:dim] + (left // 2, 2) + part.shape[dim + 1 :])
        mine = lax.dynamic_index_in_dim(pairs, bit, dim + 1, keepdims=False)
        theirs = lax.dynamic_index_in_dim(pairs, 1 - bit, dim + 1, keepdims=False)
        swap = [(k, k ^ stride) for k in range(count)]
        got = lax.ppermute(theirs.astype(jnp.bfloat16), name, swap)
        part = mine.astype(jnp.float32) + got.astype(jnp.float32)
        self.part = part.astype(jnp.bfloat16) if self.order else part
        return self.part

    def finish(self):
        while self.order:
            self.step()
        return self.part.reshape(self.rows, self.columns)


def rotated(value, axis, shift):
    count = lax.axis_size(axis)
    return lax.ppermute(value, axis, [(k, (k + shift) % count) for k in range(count)])


def scatter_sum(rows, axis):
    count, me = lax.axis_size(axis), lax.axis_index(axis)
    shares = rows.reshape(count, rows.shape[0] // count, rows.shape[1])
    total = lax.dynamic_index_in_dim(shares, me, 0, keepdims=False)
    for shift in range(1, count):
        away = lax.dynamic_index_in_dim(shares, (me + shift) % count, 0, keepdims=False)
        total = total + rotated(away, axis, shift)
    return total


def ordered_sum(rows, axis):
    shares = collected(rows, axis)
    total = shares[0]
    for share in shares[1:]:
        total = total + share
    return total


def collected(rows, axis):
    count, me = lax.axis_size(axis), lax.axis_index(axis)
    came = jnp.stack([rows] + [rotated(rows, axis, shift) for shift in range(1, count)])
    return [
        lax.dynamic_index_in_dim(came, (me - k) % count, 0, keepdims=False) for k in range(count)
    ]


def steps_of(*names):
    bits = {name: int(math.log2(lax.axis_size(name))) for name in names}
    bits["col"] -= 1
    order = ["col"]
    for name in names:
        order += [name] * bits[name]
    return order


def shards(images_in, keep, dw_weight, layer_norm_gain, w_in, w_out, layer_scale, out_grad):
    batch, tile_h, tile_w, width = images_in.shape
    cells = tile_h * tile_w
    total_rows = batch * cells
    padded = extend(images_in)
    xhat, normed, rstd = conv_norm(padded, dw_weight, layer_norm_gain)
    centered_scaled_input = xhat.reshape(total_rows, width)
    normalized_input = normed.reshape(total_rows, width)
    inverse_deviation = rstd.reshape(total_rows, 1)
    pre = jnp.dot(normalized_input, w_in, preferred_element_type=jnp.float32)
    cdf = 0.5 * (1.0 + lax.erf(pre * (1.0 / math.sqrt(2.0))))
    hidden = (pre * cdf).astype(jnp.bfloat16)
    branch = jnp.dot(hidden, w_out, preferred_element_type=jnp.float32)
    factor = jnp.repeat(keep.astype(jnp.float32) / keep_rate, cells)[:, None]
    flat_in = images_in.reshape(total_rows, width).astype(jnp.float32)
    output = (flat_in + factor * layer_scale * branch).astype(jnp.bfloat16).reshape(images_in.shape)
    upstream = out_grad.reshape(total_rows, width).astype(jnp.float32)
    g_branch = (factor * layer_scale * upstream).astype(jnp.bfloat16)
    w_out_term = jnp.dot(hidden.T, g_branch, preferred_element_type=jnp.float32).astype(jnp.bfloat16)
    w_out_share = Halving(w_out_term, steps_of("col", "row", "dp"))
    gamma_term = jnp.sum(factor * upstream * branch, axis=0)
    slope = cdf + pre * jnp.exp(-0.5 * pre * pre) * (1.0 / math.sqrt(2.0 * math.pi))
    g_pre = (jnp.dot(after(g_branch, w_out_term), w_out.T, preferred_element_type=jnp.float32) * slope).astype(
        jnp.bfloat16
    )
    normalized_gradient = jnp.dot(after(g_pre, w_out_share.step()), w_in.T, preferred_element_type=jnp.float32)
    gain_contribution = jnp.sum(normalized_gradient * centered_scaled_input, axis=0)
    input_gradient = normalized_gradient * layer_norm_gain
    convolution_gradient = (
        inverse_deviation
        * (
            input_gradient
            - jnp.mean(input_gradient, axis=-1, keepdims=True)
            - centered_scaled_input
            * jnp.mean(input_gradient * centered_scaled_input, axis=-1, keepdims=True)
        )
    ).astype(jnp.bfloat16)
    g_conv4 = convolution_gradient.reshape(batch, tile_h, tile_w, width)
    w_in_term = jnp.dot(normalized_input.T, g_pre, preferred_element_type=jnp.float32).astype(jnp.bfloat16)
    w_in_share = Halving(w_in_term, steps_of("dp", "row", "col"))
    g_tall = extend_along(g_conv4, "row", 1)
    first_half = kernel_gradient(padded, after(g_conv4, w_in_term), 0, 2)
    second_half = kernel_gradient(
        padded, after(g_conv4, first_half, g_tall, w_in_share.step()), 1, 2
    )
    g_padded = extend_along(g_tall, "col", 2)
    dw_term = jnp.concatenate([first_half, second_half], axis=1)
    taps = KERNEL * KERNEL
    small = jnp.concatenate([dw_term, gain_contribution[None], gamma_term[None]], axis=0)
    columns = lax.axis_size("col")
    padding = -small.shape[0] % (8 * columns)
    small = jnp.pad(small, ((0, padding), (0, 0)))
    flipped = dw_weight.reshape(KERNEL, KERNEL, width)[::-1, ::-1].reshape(KERNEL * KERNEL, width)
    images = jnp.float32(batch * lax.axis_size("dp"))
    front = batch // 2
    small = scatter_sum(small, "col")
    part = conv_back(
        after(g_padded, second_half, w_out_share.step()), flipped, out_grad, 0, front, None
    )
    w_in_second, w_out_third = w_in_share.step(), w_out_share.step()
    grad_input = conv_back(
        g_padded,
        flipped,
        out_grad,
        front,
        batch - front,
        after(part, small, w_in_second, w_out_third),
    )
    small = ordered_sum(after(small, part), "row")
    small = ordered_sum(after(small, grad_input), "dp")
    small = jnp.concatenate(collected(small, "col"), axis=0) / images
    dw_sum, gain_sum, gamma_sum = small[:taps], small[taps], small[taps + 1]
    w_out_sum, w_in_sum = w_out_share.finish(), w_in_share.finish()
    return (
        output,
        grad_input,
        w_in_sum / images,
        w_out_sum / images,
        dw_sum,
        gain_sum,
        gamma_sum,
    )


def solution(mesh):
    placed = (
        P("dp", "row", "col", None),
        P("dp"),
        P(),
        P(),
        P(),
        P(),
        P(),
        P("dp", "row", "col", None),
    )
    return jax.shard_map(
        shards,
        mesh=mesh,
        in_specs=placed,
        out_specs=(
            P("dp", "row", "col", None),
            P("dp", "row", "col", None),
            P(("dp", "row", "col"), None),
            P(("dp", "row", "col"), None),
            P(),
            P(),
            P(),
        ),
        check_vma=False,
    )
```

time: 377 us -> 256 us (0.68)
  waiting for transfers between devices: 175 us -> 40.1 us
  starting transfers between devices: 40 us -> 57.6 us
  between operations: 14.8 us -> 1.58 us
  Pallas kernels: 59.9 us -> 72.4 us
  other arithmetic: 25.9 us -> 16.4 us
  matrix products: 37.9 us -> 44.3 us
    psum x1 -> x0, waiting for transfers between devices: 123 us -> none  [shards(): small = lax.psum(small, ('dp', 'row', 'col')) / images]
    ppermute x18 -> x32, starting transfers between devices: 40 us -> 57.6 us  [the longest x8 20.6 us: extend(): line.append(lax.ppermute(part, ('row', 'col'), pairs))]
    pallas_call x3 -> x5, Pallas kernels: 59.9 us -> 72.4 us  [the longest x1 30.7 us: conv_norm(): pl.pallas_call(norm_kernel, grid=(batch, width // LANES), in_specs=[pl.Bl...]
    ppermute x18 -> x32, waiting for transfers between devices: 51.7 us -> 40.1 us  [the longest x10 27 us: step(): got = lax.ppermute(theirs.astype(jnp.bfloat16), name, swap)]
    reduce_sum x2 -> x0, other arithmetic: 5.2 us -> none  [the longest x1 2.74 us: shards(): jnp.mean(local_device * local_device, axis=-1, keepdims=True) + eps]
    convert_element_type x10 -> x9, other arithmetic: 9.42 us -> 5.66 us  [the longest x8 5.64 us: step(): self.part = part.astype(jnp.bfloat16) if self.order else part]
  transfers between devices with their start and end apart: 19 -> 32, of which waited for: 8 -> 9; matrix products, arithmetic and copies ran while one was open for 7% -> 20% of each run, Pallas kernels for 11% -> 16%
where the time goes in v2:
time: 256 us; the launch traced here: 255 us
  Pallas kernels  72.4 us (28%)
  starting transfers between devices  57.6 us (22%)
  matrix products  44.3 us (17%)
  waiting for transfers between devices  40.1 us (16%)
  local copies, waits for them, and re-layouts  22.6 us (9%)
  other arithmetic  16.4 us (6%)
    pallas_call x1, Pallas kernels, conv_norm(): pl.pallas_call(norm_kernel, grid=(batch, width // LANES), in_specs=[pl.Bl...  30.7 us
    ppermute x10, waiting for transfers between devices, step(): got = lax.ppermute(theirs.astype(jnp.bfloat16), name, swap)  27 us
    pallas_call x2, Pallas kernels, conv_back(): pl.pallas_call(back_kernel, grid=(width // LANES, count), in_specs=in_spe...  21 us
    pallas_call x2, Pallas kernels, kernel_gradient(): pl.pallas_call(dw_kernel, grid=(blocks, batch), in_specs=[pl.BlockSpec((1...  20.7 us
    ppermute x8, starting transfers between devices, extend(): line.append(lax.ppermute(part, ('row', 'col'), pairs))  20.6 us
    ppermute x10, starting transfers between devices, rotated(): lax.ppermute(value, axis, [(k, (k + shift) % count) for k in range(count)])  12.9 us
    ppermute x10, starting transfers between devices, step(): got = lax.ppermute(theirs.astype(jnp.bfloat16), name, swap)  11.5 us
    ppermute x2, starting transfers between devices, extend_along(): lax.ppermute(lax.slice_in_dim(field, full - width, None, axis=dim), axis,...  10 us
  transfers between devices with their start and end apart: 32, of which 9 were waited for; matrix products, arithmetic and copies ran while one was open for 20% of the time, Pallas kernels for 16%

profile of v2, /device:TPU:0, one launch (start us, length us, event | category | flops | bytes accessed | tf_op | source)
XLA Modules:
  0.0 255.1 jit_solution(164476046152457656)
XLA Ops:
  2.1 4.4 %collective-permute-start = (bf16[4,3,3,1024]{3,2,1,0:T(4,128)(2,1)S(1)}, bf16[4,3,3,1024]{3,2,1,0:T(4,128)(2,1)S(1)}, u32[]{:S(2)}, u32[]{:S(2)}) collective-permute-start(bf16[4,3,3,1024]{3,2,1,0:T(4,128)(2,1)S(1)} %get-tuple-element.41), channel_id=1, source_target_pairs={{0,5},{1,6},{2,7},{4,9},{5,10},{6,11},{8,13},{9,14},{10,15},{16,21... | collective-permute-start | bytes 221192 | tf_op jit(solution)/shard_map/ppermute | solution.py:38
  7.8 2.1 fusion.28
  9.9 7.0 %collective-permute-start.1 = (bf16[4,3,16,1024]{3,2,1,0:T(8,128)(2,1)}, bf16[4,3,16,1024]{3,2,1,0:T(8,128)(2,1)S(1)}, u32[]{:S(2)}, u32[]{:S(2)}) collective-permute-start(bf16[4,3,16,1024]{3,2,1,0:T(8,128)(2,1)} %get-tuple-element.45), channel_id=1, source_target_pairs={{0,4},{1,5},{2,6},{3,7},{4,8},{5,9},{6,10},{7,11},{8,12},{9,13},{1... | collective-permute-start | bytes 1179656 | tf_op jit(solution)/shard_map/ppermute | solution.py:38
  18.2 2.0 fusion.29
  20.2 4.0 %collective-permute-start.3 = (bf16[4,16,3,1024]{3,2,1,0:T(4,128)(2,1)S(1)}, bf16[4,16,3,1024]{3,2,1,0:T(4,128)(2,1)S(1)}, u32[]{:S(2)}, u32[]{:S(2)}) collective-permute-start(bf16[4,16,3,1024]{3,2,1,0:T(4,128)(2,1)S(1)} %get-tuple-element.47), channel_id=1, source_target_pairs={{0,1},{1,2},{2,3},{4,5},{5,6},{6,7},{8,9},{9,10},{10,11},{12,13},{... | collective-permute-start | bytes 1179656 | tf_op jit(solution)/shard_map/ppermute | solution.py:38
  27.0 6.9 %collective-permute-done.7 = bf16[4,3,3,1024]{3,2,1,0:T(4,128)(2,1)S(1)} collective-permute-done((bf16[4,3,3,1024]{3,2,1,0:T(4,128)(2,1)S(1)}, bf16[4,3,3,1024]{3,2,1,0:T(4,128)(2,1)S(1)}, u32[]{:S(2)}, u32[]{:S(2)}) %collective-permute-start.7) | collective-permute-done | bytes 73760 | tf_op jit(solution)/shard_map/ppermute | solution.py:38
  33.9 4.1 %maximum_maximum_fusion.x_ref = bf16[4,22,22,1024]{3,2,1,0:T(8,128)(2,1)S(1)} fusion(bf16[4,3,3,1024]{3,2,1,0:T(4,128)(2,1)S(1)} %collective-permute-done.7, bf16[4,3,16,1024]{3,2,1,0:T(8,128)(2,1)} %collective-permute-done.6, bf16[4,3,3,1024]{3,2,1,0:T(4,128)(2,1)S(1)} %collective-permute-done.5, bf16[4,16,3,1024]{3,2,1,0:T(4,128)(2,1)S(1)} %collective-permute-done.4, ...), kind=kLoop, calls=%fused_computation.12 | loop fusion | flops 35684352 | bytes 7929856 | tf_op jit(solution)/shard_map/concatenate | solution.py:40
  38.1 30.7 %shard_map.135 = (f32[4,16,16,1024]{3,2,1,0:T(8,128)S(1)}, bf16[4,16,16,1024]{3,2,1,0:T(8,128)(2,1)S(1)}, f32[4,16,16,1]{3,2,1,0:T(8,128)S(1)}) custom-call(bf16[4,22,22,1024]{3,2,1,0:T(8,128)(2,1)S(1)} %maximum_maximum_fusion.x_ref, f32[49,1024]{1,0:T(8,128)S(1)} %convert_element_type.174.w_ref, f32[1,1024]{1,0:T(1,128)S(1)} %bitcast.117), custom_call_target="tpu_custom_call" | custom-call | flops 15728640000 | bytes 8388608 | tf_op jit(solution)/shard_map/pallas_call | solution.py:107
  72.4 9.6 %multiply_convert_fusion = (bf16[1024,2048]{1,0:T(8,128)(2,1)S(1)}, f32[1024,2048]{1,0:T(8,128)}) fusion(bf16[1024,1024]{1,0:T(8,128)(2,1)} %bitcast.118, bf16[1024,2048]{1,0:T(8,128)(2,1)} %param.12), kind=kOutput, calls=%fused_computation.7 | convolution fusion | flops 4305453056 | bytes 18874368 | tf_op jit(solution)/shard_map/dot_general | solution.py:297
  82.0 6.8 %fusion.7 = (f32[1024]{0:T(1024)S(1)}, bf16[1024,1024]{1,0:T(8,128)(2,1)}, bf16[1024,1024]{1,0:T(8,128)(2,1)S(1)}) fusion(bf16[4,16,16,1024]{3,2,1,0:T(8,128)(2,1)S(1)} %copy-done.4, f32[1024]{0:T(1024)S(1)} %bitcast.144, f32[1024]{0:T(1024)S(1)} %copy-done.14, bf16[4,16,16,1024]{3,2,1,0:T(8,128)(2,1)S(1)} %copy-done.8, ...), kind=kOutput, calls=%fused_computation.15 | convolution fusion | flops 4306500608 | bytes 16789504 | tf_op jit(solution)/shard_map/dot_general | solution.py:300
  88.8 4.9 %convolution_convert_fusion.1 = bf16[2048,1024]{1,0:T(8,128)(2,1)S(1)} fusion(bf16[1024,2048]{1,0:T(8,128)(2,1)S(1)} %get-tuple-element.58, bf16[1024,1024]{1,0:T(8,128)(2,1)S(1)} %get-tuple-element.20), kind=kOutput, calls=%fused_computation.32 | convolution fusion | flops 4297064448 | bytes 10485760 | tf_op jit(solution)/shard_map/dot_general | solution.py:306
  94.5 3.2 %collective-permute-start.8 = (bf16[2,4,2,64,1024]{4,3,1,0,2:T(8,128)(2,1)S(1)}, bf16[2,4,2,64,1024]{4,3,1,0,2:T(8,128)(2,1)S(1)}, u32[]{:S(2)}, u32[]{:S(2)}) collective-permute-start(bf16[2,4,2,64,1024]{4,3,1,0,2:T(8,128)(2,1)S(1)} %bitcast.127), channel_id=1, source_target_pairs={{0,1},{1,0},{2,3},{3,2},{4,5},{5,4},{6,7},{7,6},{8,9},{9,8},{10,11... | collective-permute-start | bytes 6291464 | tf_op jit(solution)/shard_map/ppermute | solution.py:237
  97.6 9.0 %fusion.5 = bf16[1024,2048]{1,0:T(8,128)(2,1)S(1)} fusion(f32[1024,2048]{1,0:T(8,128)} %get-tuple-element.59, bf16[1024,1024]{1,0:T(8,128)(2,1)S(1)} %get-tuple-element.20, bf16[2048,1024]{1,0:T(8,128)(2,1)S(1)} %copy-done.13), kind=kOutput, calls=%fused_computation.6 | convolution fusion | flops 4315938816 | bytes 18874368 | tf_op jit(solution)/shard_map/dot_general | solution.py:310
  106.7 5.1 %convolution_convert_fusion = bf16[1024,2048]{1,0:T(8,128)(2,1)S(1)} fusion(bf16[1024,1024]{1,0:T(8,128)(2,1)S(1)} %bitcast.119, bf16[1024,2048]{1,0:T(8,128)(2,1)S(1)} %fusion.5), kind=kOutput, calls=%fused_computation.31 | convolution fusion | flops 4297064448 | bytes 10485760 | tf_op jit(solution)/shard_map/dot_general | solution.py:326
  114.6 8.9 %fusion.17 = (f32[1024]{0:T(1024)S(1)}, f32[1024]{0:T(1024)S(1)}, f32[1024]{0:T(1024)S(1)}, f32[1024,1024]{1,0:T(8,128)S(1)}) fusion(f32[4,16,16,1024]{3,2,1,0:T(8,128)S(1)} %copy-done.2, f32[1024]{0:T(1024)S(1)} %copy-done.3, bf16[1024,2048]{1,0:T(8,128)(2,1)} %copy-done.16, bf16[1024,2048]{1,0:T(8,128)(2,1)} %param.12), kind=kOutput, calls=%fused_computation.30 | convolution fusion | flops 4301255680 | bytes 16793600 | tf_op jit(solution)/shard_map/dot_general | solution.py:313
  125.1 4.6 %collective-permute-start.9 = (bf16[4,3,16,1024]{3,2,1,0:T(8,128)(2,1)S(1)}, bf16[4,3,16,1024]{3,2,1,0:T(8,128)(2,1)S(1)}, u32[]{:S(2)}, u32[]{:S(2)}) collective-permute-start(bf16[4,3,16,1024]{3,2,1,0:T(8,128)(2,1)S(1)} %get-tuple-element.39), channel_id=1, source_target_pairs={{0,4},{4,8},{8,12},{1,5},{5,9},{9,13},{2,6},{6,10},{10,14},{3,7},{... | collective-permute-start | bytes 1179656 | tf_op jit(solution)/shard_map/ppermute | solution.py:47
  132.1 10.3 %shard_map.136 = f32[49,512]{1,0:T(8,128)S(1)} custom-call(bf16[4,22,22,1024]{3,2,1,0:T(8,128)(2,1)S(1)} %bitcast.116, bf16[4,16,16,1024]{3,2,1,0:T(8,128)(2,1)S(1)} %bitcast.111), custom_call_target="tpu_custom_call" | custom-call | flops 7864320000 | bytes 3145728 | tf_op jit(solution)/shard_map/pallas_call | solution.py:198
  142.4 2.1 fusion.11
  145.0 10.3 %shard_map.137 = f32[49,512]{1,0:T(8,128)S(1)} custom-call(bf16[4,22,22,1024]{3,2,1,0:T(8,128)(2,1)S(1)} %bitcast.116, bf16[4,16,16,1024]{3,2,1,0:T(8,128)(2,1)S(1)} %bitcast.113), custom_call_target="tpu_custom_call" | custom-call | flops 7864320000 | bytes 3145728 | tf_op jit(solution)/shard_map/pallas_call | solution.py:198
  160.6 5.5 %collective-permute-start.11 = (bf16[4,22,3,1024]{3,0,2,1:T(4,128)(2,1)}, bf16[4,22,3,1024]{3,0,2,1:T(4,128)(2,1)}, u32[]{:S(2)}, u32[]{:S(2)}) collective-permute-start(bf16[4,22,3,1024]{3,0,2,1:T(4,128)(2,1)} %copy.21), channel_id=1, source_target_pairs={{0,1},{1,2},{2,3},{4,5},{5,6},{6,7},{8,9},{9,10},{10,11},{12,13},{... | collective-permute-start | bytes 1622024 | tf_op jit(solution)/shard_map/ppermute | solution.py:47
  166.7 3.0 %collective-permute-start.16 = (f32[16,1024]{1,0:T(8,128)}, f32[16,1024]{1,0:T(8,128)S(1)}, u32[]{:S(2)}, u32[]{:S(2)}) collective-permute-start(f32[16,1024]{1,0:T(8,128)} %get-tuple-element.57), channel_id=1, source_target_pairs={{0,2},{1,3},{2,0},{3,1},{4,6},{5,7},{6,4},{7,5},{8,10},{9,11},{10,... | collective-permute-start | bytes 196616 | tf_op jit(solution)/shard_map/ppermute | solution.py:250
  176.2 2.9 %pad_maximum_fusion.x_ref = bf16[4,22,22,1024]{3,2,1,0:T(8,128)(2,1)S(1)} fusion(bf16[4,22,3,1024]{3,2,1,0:T(4,128)(2,1)S(1)} %copy.24, bf16[4,3,16,1024]{3,2,1,0:T(8,128)(2,1)S(1)} %collective-permute-done.10, bf16[4,16,16,1024]{3,2,1,0:T(8,128)(2,1)S(1)} %bitcast.114, bf16[4,3,16,1024]{3,2,1,0:T(8,128)(2,1)S(1)} %collective-permute-done.9, ...), kind=kLoop, calls=%fused_computation.13 | loop fusion | flops 19824640 | bytes 7929856 | tf_op jit(solution)/shard_map/concatenate | solution.py:49
  180.8 10.5 %shard_map.138.rest_0_ = bf16[4,16,16,1024]{3,2,1,0:T(8,128)(2,1)} custom-call(bf16[4,22,22,1024]{3,2,1,0:T(8,128)(2,1)S(1)} %pad_maximum_fusion.x_ref, f32[49,1024]{1,0:T(8,128)S(1)} %reshape.155.w_ref, bf16[4,16,16,1024]{3,2,1,0:T(8,128)(2,1)S(1)} %copy-done.5), custom_call_target="tpu_custom_call" | custom-call | flops 7864320000 | bytes 3145728 | tf_op jit(solution)/shard_map/pallas_call | solution.py:156
  191.3 3.0 %collective-permute-start.27 = (f32[16,1024]{1,0:T(8,128)S(1)}, f32[16,1024]{1,0:T(8,128)S(1)}, u32[]{:S(2)}, u32[]{:S(2)}) collective-permute-start(f32[16,1024]{1,0:T(8,128)S(1)} %fusion.24), channel_id=1, source_target_pairs={{0,12},{4,0},{8,4},{12,8},{1,13},{5,1},{9,5},{13,9},{2,14},{6,2},{... | collective-permute-start | bytes 196616 | tf_op jit(solution)/shard_map/ppermute | solution.py:250
  200.0 2.6 %collective-permute-done.26 = f32[16,1024]{1,0:T(8,128)S(1)} collective-permute-done((f32[16,1024]{1,0:T(8,128)S(1)}, f32[16,1024]{1,0:T(8,128)S(1)}, u32[]{:S(2)}, u32[]{:S(2)}) %collective-permute-start.26) | collective-permute-done | bytes 65568 | tf_op jit(solution)/shard_map/ppermute | solution.py:250
  202.7 11.2 %collective-permute-done.19 = bf16[2,2,1,64,1024]{4,3,1,0,2:T(8,128)(2,1)S(1)} collective-permute-done((bf16[2,2,1,64,1024]{4,3,1,0,2:T(8,128)(2,1)S(1)}, bf16[2,2,1,64,1024]{4,3,1,0,2:T(8,128)(2,1)S(1)}, u32[]{:S(2)}, u32[]{:S(2)}) %collective-permute-start.19) | collective-permute-done | bytes 524320 | tf_op jit(solution)/shard_map/ppermute | solution.py:237
  214.2 10.5 %shard_map.139 = bf16[4,16,16,1024]{3,2,1,0:T(8,128)(2,1)} custom-call(bf16[4,22,22,1024]{3,2,1,0:T(8,128)(2,1)S(1)} %pad_maximum_fusion.x_ref, f32[49,1024]{1,0:T(8,128)S(1)} %reshape.155.w_ref, bf16[4,16,16,1024]{3,2,1,0:T(8,128)(2,1)S(1)} %copy-done.5, bf16[4,16,16,1024]{3,2,1,0:T(8,128)(2,1)} %shard_map.138.rest_0_), custom_call_target="tpu_custom_call", output_to_operand_aliasing={{}: (3, {})} | custom-call | flops 7864320000 | bytes 3145728 | tf_op jit(solution)/shard_map/pallas_call | solution.py:156
  226.2 4.5 %collective-permute-done.20 = bf16[1,2,2,32,2048]{4,3,2,1,0:T(8,128)(2,1)S(1)} collective-permute-done((bf16[1,2,2,32,2048]{4,3,2,1,0:T(8,128)(2,1)S(1)}, bf16[1,2,2,32,2048]{4,3,2,1,0:T(8,128)(2,1)S(1)}, u32[]{:S(2)}, u32[]{:S(2)}) %collective-permute-start.20) | collective-permute-done | bytes 524320 | tf_op jit(solution)/shard_map/ppermute | solution.py:237
  230.9 2.4 collective-permute-start.31
  235.6 2.4 collective-permute-done.30
  241.1 7.6 %collective-permute-done.21 = bf16[1,1,2,32,2048]{4,3,2,1,0:T(8,128)(2,1)S(1)} collective-permute-done((bf16[1,1,2,32,2048]{4,3,2,1,0:T(8,128)(2,1)S(1)}, bf16[1,1,2,32,2048]{4,3,2,1,0:T(8,128)(2,1)S(1)}, u32[]{:S(2)}, u32[]{:S(2)}) %collective-permute-start.21) | collective-permute-done | bytes 262176 | tf_op jit(solution)/shard_map/ppermute | solution.py:237
  250.7 3.7 %collective-permute-done.22 = bf16[1,1,1,32,2048]{4,3,2,1,0:T(8,128)(2,1)S(1)} collective-permute-done((bf16[1,1,1,32,2048]{4,3,2,1,0:T(8,128)(2,1)S(1)}, bf16[1,1,1,32,2048]{4,3,2,1,0:T(8,128)(2,1)S(1)}, u32[]{:S(2)}, u32[]{:S(2)}) %collective-permute-start.22) | collective-permute-done | bytes 131104 | tf_op jit(solution)/shard_map/ppermute | solution.py:237
  (137 shorter events, 47.8 us)
Async XLA Ops:
  2.1 18.1 %collective-permute-start = (bf16[4,3,3,1024]{3,2,1,0:T(4,128)(2,1)S(1)}, bf16[4,3,3,1024]{3,2,1,0:T(4,128)(2,1)S(1)}, u32[]{:S(2)}, u32[]{:S(2)}) collective-permute-start(bf16[4,3,3,1024]{3,2,1,0:T(4,128)(2,1)S(1)} %get-tuple-element.41), channel_id=1, source_target_pairs={{0,5},{1,6},{2,7},{4,9},{5,10},{6,11},{8,13},{9,14},{10,15},{16,21... | collective-permute-start | bytes 221192 | tf_op jit(solution)/shard_map/ppermute | solution.py:38
  6.5 17.8 %collective-permute-start.5 = (bf16[4,3,3,1024]{3,2,1,0:T(4,128)(2,1)S(1)}, bf16[4,3,3,1024]{3,2,1,0:T(4,128)(2,1)S(1)}, u32[]{:S(2)}, u32[]{:S(2)}) collective-permute-start(bf16[4,3,3,1024]{3,2,1,0:T(4,128)(2,1)S(1)} %get-tuple-element.42), channel_id=1, source_target_pairs={{4,1},{5,2},{6,3},{8,5},{9,6},{10,7},{12,9},{13,10},{14,11},{20,17... | collective-permute-start | bytes 221192 | tf_op jit(solution)/shard_map/ppermute | solution.py:38
  7.1 18.4 %collective-permute-start.2 = (bf16[4,3,3,1024]{3,2,1,0:T(4,128)(2,1)S(1)}, bf16[4,3,3,1024]{3,2,1,0:T(4,128)(2,1)S(1)}, u32[]{:S(2)}, u32[]{:S(2)}) collective-permute-start(bf16[4,3,3,1024]{3,2,1,0:T(4,128)(2,1)S(1)} %get-tuple-element.43), channel_id=1, source_target_pairs={{1,4},{2,5},{3,6},{5,8},{6,9},{7,10},{9,12},{10,13},{11,14},{17,20... | collective-permute-start | bytes 221192 | tf_op jit(solution)/shard_map/ppermute | solution.py:38
  9.9 24.0 %collective-permute-start.1 = (bf16[4,3,16,1024]{3,2,1,0:T(8,128)(2,1)}, bf16[4,3,16,1024]{3,2,1,0:T(8,128)(2,1)S(1)}, u32[]{:S(2)}, u32[]{:S(2)}) collective-permute-start(bf16[4,3,16,1024]{3,2,1,0:T(8,128)(2,1)} %get-tuple-element.45), channel_id=1, source_target_pairs={{0,4},{1,5},{2,6},{3,7},{4,8},{5,9},{6,10},{7,11},{8,12},{9,13},{1... | collective-permute-start | bytes 1179656 | tf_op jit(solution)/shard_map/ppermute | solution.py:38
  16.9 17.0 %collective-permute-start.6 = (bf16[4,3,16,1024]{3,2,1,0:T(8,128)(2,1)}, bf16[4,3,16,1024]{3,2,1,0:T(8,128)(2,1)}, u32[]{:S(2)}, u32[]{:S(2)}) collective-permute-start(bf16[4,3,16,1024]{3,2,1,0:T(8,128)(2,1)} %get-tuple-element.46), channel_id=1, source_target_pairs={{4,0},{5,1},{6,2},{7,3},{8,4},{9,5},{10,6},{11,7},{12,8},{13,9},{1... | collective-permute-start | bytes 1179656 | tf_op jit(solution)/shard_map/ppermute | solution.py:38
  20.2 13.7 %collective-permute-start.3 = (bf16[4,16,3,1024]{3,2,1,0:T(4,128)(2,1)S(1)}, bf16[4,16,3,1024]{3,2,1,0:T(4,128)(2,1)S(1)}, u32[]{:S(2)}, u32[]{:S(2)}) collective-permute-start(bf16[4,16,3,1024]{3,2,1,0:T(4,128)(2,1)S(1)} %get-tuple-element.47), channel_id=1, source_target_pairs={{0,1},{1,2},{2,3},{4,5},{5,6},{6,7},{8,9},{9,10},{10,11},{12,13},{... | collective-permute-start | bytes 1179656 | tf_op jit(solution)/shard_map/ppermute | solution.py:38
  24.2 9.7 %collective-permute-start.4 = (bf16[4,16,3,1024]{3,2,1,0:T(4,128)(2,1)S(1)}, bf16[4,16,3,1024]{3,2,1,0:T(4,128)(2,1)S(1)}, u32[]{:S(2)}, u32[]{:S(2)}) collective-permute-start(bf16[4,16,3,1024]{3,2,1,0:T(4,128)(2,1)S(1)} %get-tuple-element.48), channel_id=1, source_target_pairs={{1,0},{2,1},{3,2},{5,4},{6,5},{7,6},{9,8},{10,9},{11,10},{13,12},{... | collective-permute-start | bytes 1179656 | tf_op jit(solution)/shard_map/ppermute | solution.py:38
  25.5 8.4 %collective-permute-start.7 = (bf16[4,3,3,1024]{3,2,1,0:T(4,128)(2,1)S(1)}, bf16[4,3,3,1024]{3,2,1,0:T(4,128)(2,1)S(1)}, u32[]{:S(2)}, u32[]{:S(2)}) collective-permute-start(bf16[4,3,3,1024]{3,2,1,0:T(4,128)(2,1)S(1)} %get-tuple-element.44), channel_id=1, source_target_pairs={{5,0},{6,1},{7,2},{9,4},{10,5},{11,6},{13,8},{14,9},{15,10},{21,16... | collective-permute-start | bytes 221192 | tf_op jit(solution)/shard_map/ppermute | solution.py:38
  94.5 17.7 %collective-permute-start.8 = (bf16[2,4,2,64,1024]{4,3,1,0,2:T(8,128)(2,1)S(1)}, bf16[2,4,2,64,1024]{4,3,1,0,2:T(8,128)(2,1)S(1)}, u32[]{:S(2)}, u32[]{:S(2)}) collective-permute-start(bf16[2,4,2,64,1024]{4,3,1,0,2:T(8,128)(2,1)S(1)} %bitcast.127), channel_id=1, source_target_pairs={{0,1},{1,0},{2,3},{3,2},{4,5},{5,4},{6,7},{7,6},{8,9},{9,8},{10,11... | collective-permute-start | bytes 6291464 | tf_op jit(solution)/shard_map/ppermute | solution.py:237
  112.1 30.4 %collective-permute-start.13 = (bf16[2,4,2,32,2048]{4,3,2,1,0:T(8,128)(2,1)S(1)}, bf16[2,4,2,32,2048]{4,3,2,1,0:T(8,128)(2,1)S(1)}, u32[]{:S(2)}, u32[]{:S(2)}) collective-permute-start(bf16[2,4,2,32,2048]{4,3,2,1,0:T(8,128)(2,1)S(1)} %dynamic-slice_bitcast_fusion), channel_id=1, source_target_pairs={{0,1},{1,0},{2,3},{3,2},{4,5},{5,4},{6,7},{7,6},{8,9},{9,8},{10,11... | collective-permute-start | bytes 6291464 | tf_op jit(solution)/shard_map/ppermute | solution.py:237
  125.1 19.5 %collective-permute-start.9 = (bf16[4,3,16,1024]{3,2,1,0:T(8,128)(2,1)S(1)}, bf16[4,3,16,1024]{3,2,1,0:T(8,128)(2,1)S(1)}, u32[]{:S(2)}, u32[]{:S(2)}) collective-permute-start(bf16[4,3,16,1024]{3,2,1,0:T(8,128)(2,1)S(1)} %get-tuple-element.39), channel_id=1, source_target_pairs={{0,4},{4,8},{8,12},{1,5},{5,9},{9,13},{2,6},{6,10},{10,14},{3,7},{... | collective-permute-start | bytes 1179656 | tf_op jit(solution)/shard_map/ppermute | solution.py:47
  129.7 14.9 %collective-permute-start.10 = (bf16[4,3,16,1024]{3,2,1,0:T(8,128)(2,1)S(1)}, bf16[4,3,16,1024]{3,2,1,0:T(8,128)(2,1)S(1)}, u32[]{:S(2)}, u32[]{:S(2)}) collective-permute-start(bf16[4,3,16,1024]{3,2,1,0:T(8,128)(2,1)S(1)} %get-tuple-element.40), channel_id=1, source_target_pairs={{4,0},{8,4},{12,8},{5,1},{9,5},{13,9},{6,2},{10,6},{14,10},{7,3},{... | collective-permute-start | bytes 1179656 | tf_op jit(solution)/shard_map/ppermute | solution.py:48
  132.1 47.0 %collective-permute-start.14 = (bf16[2,4,1,64,1024]{4,3,1,0,2:T(8,128)(2,1)}, bf16[2,4,1,64,1024]{4,3,1,0,2:T(8,128)(2,1)}, u32[]{:S(2)}, u32[]{:S(2)}) collective-permute-start(bf16[2,4,1,64,1024]{4,3,1,0,2:T(8,128)(2,1)} %constant_dynamic-slice_fusion.5), channel_id=1, source_target_pairs={{0,2},{1,3},{2,0},{3,1},{4,6},{5,7},{6,4},{7,5},{8,10},{9,11},{10,... | collective-permute-start | bytes 3145736 | tf_op jit(solution)/shard_map/ppermute | solution.py:237
  156.0 10.7 %collective-permute-start.15 = (f32[16,1024]{1,0:T(8,128)}, f32[16,1024]{1,0:T(8,128)S(1)}, u32[]{:S(2)}, u32[]{:S(2)}) collective-permute-start(f32[16,1024]{1,0:T(8,128)} %get-tuple-element.55), channel_id=1, source_target_pairs={{0,1},{1,2},{2,3},{3,0},{4,5},{5,6},{6,7},{7,4},{8,9},{9,10},{10,1... | collective-permute-start | bytes 196616 | tf_op jit(solution)/shard_map/ppermute | solution.py:250
  158.0 15.3 %collective-permute-start.12 = (bf16[4,22,3,1024]{3,0,2,1:T(4,128)(2,1)}, bf16[4,22,3,1024]{3,0,2,1:T(4,128)(2,1)}, u32[]{:S(2)}, u32[]{:S(2)}) collective-permute-start(bf16[4,22,3,1024]{3,0,2,1:T(4,128)(2,1)} %copy.22), channel_id=1, source_target_pairs={{1,0},{2,1},{3,2},{5,4},{6,5},{7,6},{9,8},{10,9},{11,10},{13,12},{... | collective-permute-start | bytes 1622024 | tf_op jit(solution)/shard_map/ppermute | solution.py:48
  160.6 14.1 %collective-permute-start.11 = (bf16[4,22,3,1024]{3,0,2,1:T(4,128)(2,1)}, bf16[4,22,3,1024]{3,0,2,1:T(4,128)(2,1)}, u32[]{:S(2)}, u32[]{:S(2)}) collective-permute-start(bf16[4,22,3,1024]{3,0,2,1:T(4,128)(2,1)} %copy.21), channel_id=1, source_target_pairs={{0,1},{1,2},{2,3},{4,5},{5,6},{6,7},{8,9},{9,10},{10,11},{12,13},{... | collective-permute-start | bytes 1622024 | tf_op jit(solution)/shard_map/ppermute | solution.py:47
  166.6 4.4 %collective-permute-start.17 = (f32[16,1024]{1,0:T(8,128)}, f32[16,1024]{1,0:T(8,128)S(1)}, u32[]{:S(2)}, u32[]{:S(2)}) collective-permute-start(f32[16,1024]{1,0:T(8,128)} %get-tuple-element.56), channel_id=1, source_target_pairs={{0,3},{1,0},{2,1},{3,2},{4,7},{5,4},{6,5},{7,6},{8,11},{9,8},{10,9... | collective-permute-start | bytes 196616 | tf_op jit(solution)/shard_map/ppermute | solution.py:250
  166.7 6.5 %collective-permute-start.16 = (f32[16,1024]{1,0:T(8,128)}, f32[16,1024]{1,0:T(8,128)S(1)}, u32[]{:S(2)}, u32[]{:S(2)}) collective-permute-start(f32[16,1024]{1,0:T(8,128)} %get-tuple-element.57), channel_id=1, source_target_pairs={{0,2},{1,3},{2,0},{3,1},{4,6},{5,7},{6,4},{7,5},{8,10},{9,11},{10,... | collective-permute-start | bytes 196616 | tf_op jit(solution)/shard_map/ppermute | solution.py:250
  171.0 26.8 %collective-permute-start.18 = (bf16[1,4,2,32,2048]{4,3,2,1,0:T(8,128)(2,1)S(1)}, bf16[1,4,2,32,2048]{4,3,2,1,0:T(8,128)(2,1)S(1)}, u32[]{:S(2)}, u32[]{:S(2)}) collective-permute-start(bf16[1,4,2,32,2048]{4,3,2,1,0:T(8,128)(2,1)S(1)} %constant_dynamic-slice_fusion.4), channel_id=1, source_target_pairs={{0,16},{16,0},{1,17},{17,1},{2,18},{18,2},{3,19},{19,3},{4,20},{20... | collective-permute-start | bytes 3145736 | tf_op jit(solution)/shard_map/ppermute | solution.py:237
  191.3 8.7 %collective-permute-start.27 = (f32[16,1024]{1,0:T(8,128)S(1)}, f32[16,1024]{1,0:T(8,128)S(1)}, u32[]{:S(2)}, u32[]{:S(2)}) collective-permute-start(f32[16,1024]{1,0:T(8,128)S(1)} %fusion.24), channel_id=1, source_target_pairs={{0,12},{4,0},{8,4},{12,8},{1,13},{5,1},{9,5},{13,9},{2,14},{6,2},{... | collective-permute-start | bytes 196616 | tf_op jit(solution)/shard_map/ppermute | solution.py:250
  194.3 8.3 %collective-permute-start.26 = (f32[16,1024]{1,0:T(8,128)S(1)}, f32[16,1024]{1,0:T(8,128)S(1)}, u32[]{:S(2)}, u32[]{:S(2)}) collective-permute-start(f32[16,1024]{1,0:T(8,128)S(1)} %fusion.24), channel_id=1, source_target_pairs={{0,8},{4,12},{8,0},{12,4},{1,9},{5,13},{9,1},{13,5},{2,10},{6,14},... | collective-permute-start | bytes 196616 | tf_op jit(solution)/shard_map/ppermute | solution.py:250
  195.4 7.2 %collective-permute-start.25 = (f32[16,1024]{1,0:T(8,128)S(1)}, f32[16,1024]{1,0:T(8,128)S(1)}, u32[]{:S(2)}, u32[]{:S(2)}) collective-permute-start(f32[16,1024]{1,0:T(8,128)S(1)} %fusion.24), channel_id=1, source_target_pairs={{0,4},{4,8},{8,12},{12,0},{1,5},{5,9},{9,13},{13,1},{2,6},{6,10},{... | collective-permute-start | bytes 196616 | tf_op jit(solution)/shard_map/ppermute | solution.py:250
  196.9 17.0 %collective-permute-start.19 = (bf16[2,2,1,64,1024]{4,3,1,0,2:T(8,128)(2,1)S(1)}, bf16[2,2,1,64,1024]{4,3,1,0,2:T(8,128)(2,1)S(1)}, u32[]{:S(2)}, u32[]{:S(2)}) collective-permute-start(bf16[2,2,1,64,1024]{4,3,1,0,2:T(8,128)(2,1)S(1)} %dynamic-slice_bitcast_fusion.2), channel_id=1, source_target_pairs={{0,4},{4,0},{8,12},{12,8},{1,5},{5,1},{9,13},{13,9},{2,6},{6,2},{1... | collective-permute-start | bytes 1572872 | tf_op jit(solution)/shard_map/ppermute | solution.py:237
  198.3 32.4 %collective-permute-start.20 = (bf16[1,2,2,32,2048]{4,3,2,1,0:T(8,128)(2,1)S(1)}, bf16[1,2,2,32,2048]{4,3,2,1,0:T(8,128)(2,1)S(1)}, u32[]{:S(2)}, u32[]{:S(2)}) collective-permute-start(bf16[1,2,2,32,2048]{4,3,2,1,0:T(8,128)(2,1)S(1)} %dynamic-slice_bitcast_fusion.1), channel_id=1, source_target_pairs={{0,4},{4,0},{8,12},{12,8},{1,5},{5,1},{9,13},{13,9},{2,6},{6,2},{1... | collective-permute-start | bytes 1572872 | tf_op jit(solution)/shard_map/ppermute | solution.py:237
  214.1 25.3 %collective-permute-start.23 = (bf16[2,1,1,64,1024]{4,3,1,0,2:T(8,128)(2,1)S(1)}, bf16[2,1,1,64,1024]{4,3,1,0,2:T(8,128)(2,1)S(1)}, u32[]{:S(2)}, u32[]{:S(2)}) collective-permute-start(bf16[2,1,1,64,1024]{4,3,1,0,2:T(8,128)(2,1)S(1)} %constant_dynamic-slice_fusion.1), channel_id=1, source_target_pairs={{0,8},{4,12},{8,0},{12,4},{1,9},{5,13},{9,1},{13,5},{2,10},{6,14},... | collective-permute-start | bytes 786440 | tf_op jit(solution)/shard_map/ppermute | solution.py:237
  224.7 6.2 %collective-permute-start.28 = (f32[16,1024]{1,0:T(8,128)S(1)}, f32[16,1024]{1,0:T(8,128)S(1)}, u32[]{:S(2)}, u32[]{:S(2)}) collective-permute-start(f32[16,1024]{1,0:T(8,128)S(1)} %add_bitcast_fusion), channel_id=1, source_target_pairs={{0,16},{16,0},{1,17},{17,1},{2,18},{18,2},{3,19},{19,3},{4,20},{20... | collective-permute-start | bytes 196616 | tf_op jit(solution)/shard_map/ppermute | solution.py:250
  230.9 4.7 %collective-permute-start.31 = (f32[16,1024]{1,0:T(8,128)S(1)}, f32[16,1024]{1,0:T(8,128)S(1)}, u32[]{:S(2)}, u32[]{:S(2)}) collective-permute-start(f32[16,1024]{1,0:T(8,128)S(1)} %bitcast.132), channel_id=1, source_target_pairs={{0,3},{1,0},{2,1},{3,2},{4,7},{5,4},{6,5},{7,6},{8,11},{9,8},{10,9... | collective-permute-start | bytes 196616 | tf_op jit(solution)/shard_map/ppermute | solution.py:250
  233.2 4.7 %collective-permute-start.30 = (f32[16,1024]{1,0:T(8,128)S(1)}, f32[16,1024]{1,0:T(8,128)S(1)}, u32[]{:S(2)}, u32[]{:S(2)}) collective-permute-start(f32[16,1024]{1,0:T(8,128)S(1)} %bitcast.133), channel_id=1, source_target_pairs={{0,2},{1,3},{2,0},{3,1},{4,6},{5,7},{6,4},{7,5},{8,10},{9,11},{10,... | collective-permute-start | bytes 196616 | tf_op jit(solution)/shard_map/ppermute | solution.py:250
  233.6 4.4 %collective-permute-start.29 = (f32[16,1024]{1,0:T(8,128)S(1)}, f32[16,1024]{1,0:T(8,128)S(1)}, u32[]{:S(2)}, u32[]{:S(2)}) collective-permute-start(f32[16,1024]{1,0:T(8,128)S(1)} %bitcast.134), channel_id=1, source_target_pairs={{0,1},{1,2},{2,3},{3,0},{4,5},{5,6},{6,7},{7,4},{8,9},{9,10},{10,1... | collective-permute-start | bytes 196616 | tf_op jit(solution)/shard_map/ppermute | solution.py:250
  233.8 14.9 %collective-permute-start.21 = (bf16[1,1,2,32,2048]{4,3,2,1,0:T(8,128)(2,1)S(1)}, bf16[1,1,2,32,2048]{4,3,2,1,0:T(8,128)(2,1)S(1)}, u32[]{:S(2)}, u32[]{:S(2)}) collective-permute-start(bf16[1,1,2,32,2048]{4,3,2,1,0:T(8,128)(2,1)S(1)} %constant_dynamic-slice_fusion.3), channel_id=1, source_target_pairs={{0,8},{4,12},{8,0},{12,4},{1,9},{5,13},{9,1},{13,5},{2,10},{6,14},... | collective-permute-start | bytes 786440 | tf_op jit(solution)/shard_map/ppermute | solution.py:237
  239.5 10.4 %collective-permute-start.24 = (bf16[1,1,1,64,1024]{4,3,1,0,2:T(8,128)(2,1)S(1)}, bf16[1,1,1,64,1024]{4,3,1,0,2:T(8,128)(2,1)S(1)}, u32[]{:S(2)}, u32[]{:S(2)}) collective-permute-start(bf16[1,1,1,64,1024]{4,3,1,0,2:T(8,128)(2,1)S(1)} %constant_dynamic-slice_fusion), channel_id=1, source_target_pairs={{0,16},{16,0},{1,17},{17,1},{2,18},{18,2},{3,19},{19,3},{4,20},{20... | collective-permute-start | bytes 393224 | tf_op jit(solution)/shard_map/ppermute | solution.py:237
  248.8 5.6 %collective-permute-start.22 = (bf16[1,1,1,32,2048]{4,3,2,1,0:T(8,128)(2,1)S(1)}, bf16[1,1,1,32,2048]{4,3,2,1,0:T(8,128)(2,1)S(1)}, u32[]{:S(2)}, u32[]{:S(2)}) collective-permute-start(bf16[1,1,1,32,2048]{4,3,2,1,0:T(8,128)(2,1)S(1)} %constant_dynamic-slice_fusion.2), channel_id=1, source_target_pairs={{0,2},{1,3},{2,0},{3,1},{4,6},{5,7},{6,4},{7,5},{8,10},{9,11},{10,... | collective-permute-start | bytes 393224 | tf_op jit(solution)/shard_map/ppermute | solution.py:237
  (19 other events, 231.5 us)

commit v3 on v2

--- a/solution.py
+++ b/solution.py
@@ -12,32 +12,6 @@
 
 eps = 1e-06
 keep_rate = 0.75
-
-
-def extend(field, width=KERNEL // 2):
-    rows, cols = lax.axis_size("row"), lax.axis_size("col")
-    pieces = []
-    for down in (-1, 0, 1):
-        line = []
-        for right in (-1, 0, 1):
-            if down == 0 and right == 0:
-                line.append(field)
-                continue
-            part = field
-            for step, dim in ((down, 1), (right, 2)):
-                full = field.shape[dim]
-                if step == -1:
-                    part = lax.slice_in_dim(part, full - width, None, axis=dim)
-                elif step == 1:
-                    part = lax.slice_in_dim(part, 0, width, axis=dim)
-            pairs = []
-            for r in range(rows):
-                for c in range(cols):
-                    if 0 <= r + down < rows and 0 <= c + right < cols:
-                        pairs.append(((r + down) * cols + c + right, r * cols + c))
-            line.append(lax.ppermute(part, ("row", "col"), pairs))
-        pieces.append(line)
-    return jnp.concatenate([jnp.concatenate(line, axis=2) for line in pieces], axis=1)
 
 
 def extend_along(field, axis, dim, width=KERNEL // 2):
@@ -83,19 +57,24 @@
     def _():
         blocks = width // LANES
 
-        @pl.loop(0, tile_h)
+        @pl.loop(0, tile_h, step=half)
         def _(row):
-            conv = [held[block, row] for block in range(blocks)]
-            mean = jnp.sum(sum(conv), axis=-1, keepdims=True) / width
-            centred = [part - mean for part in conv]
-            spread = jnp.sum(sum(part * part for part in centred), axis=-1, keepdims=True)
-            rstd = lax.rsqrt(spread / width + eps)
-            rstd_ref[0, row] = rstd
+            rows = pl.ds(row, half)
+            total = held[0, rows]
+            for block in range(1, blocks):
+                total = total + held[block, rows]
+            mean = jnp.sum(total, axis=-1, keepdims=True) / width
+            spread = jnp.zeros_like(total)
+            for block in range(blocks):
+                centred = held[block, rows] - mean
+                spread = spread + centred * centred
+            rstd = lax.rsqrt(jnp.sum(spread, axis=-1, keepdims=True) / width + eps)
+            rstd_ref[0, rows] = rstd
             for block in range(blocks):
                 lanes = slice(block * LANES, (block + 1) * LANES)
-                xhat = centred[block] * rstd
-                xhat_ref[0, row, :, lanes] = xhat
-                normed_ref[0, row, :, lanes] = (xhat * gain_ref[:, lanes]).astype(jnp.bfloat16)
+                xhat = (held[block, rows] - mean) * rstd
+                xhat_ref[0, rows, :, lanes] = xhat
+                normed_ref[0, rows, :, lanes] = (xhat * gain_ref[:, lanes][None]).astype(jnp.bfloat16)
 
 
 def conv_norm(padded, weights, gain):
@@ -245,35 +224,9 @@
         return self.part.reshape(self.rows, self.columns)
 
 
-def rotated(value, axis, shift):
+def doubled(rows, axis, bit):
     count = lax.axis_size(axis)
-    return lax.ppermute(value, axis, [(k, (k + shift) % count) for k in range(count)])
-
-
-def scatter_sum(rows, axis):
-    count, me = lax.axis_size(axis), lax.axis_index(axis)
-    shares = rows.reshape(count, rows.shape[0] // count, rows.shape[1])
-    total = lax.dynamic_index_in_dim(shares, me, 0, keepdims=False)
-    for shift in range(1, count):
-        away = lax.dynamic_index_in_dim(shares, (me + shift) % count, 0, keepdims=False)
-        total = total + rotated(away, axis, shift)
-    return total
-
-
-def ordered_sum(rows, axis):
-    shares = collected(rows, axis)
-    total = shares[0]
-    for share in shares[1:]:
-        total = total + share
-    return total
-
-
-def collected(rows, axis):
-    count, me = lax.axis_size(axis), lax.axis_index(axis)
-    came = jnp.stack([rows] + [rotated(rows, axis, shift) for shift in range(1, count)])
-    return [
-        lax.dynamic_index_in_dim(came, (me - k) % count, 0, keepdims=False) for k in range(count)
-    ]
+    return rows + lax.ppermute(rows, axis, [(k, k ^ (1 << bit)) for k in range(count)])
 
 
 def steps_of(*names):
@@ -289,7 +242,7 @@
     batch, tile_h, tile_w, width = images_in.shape
     cells = tile_h * tile_w
     total_rows = batch * cells
-    padded = extend(images_in)
+    padded = extend_along(extend_along(images_in, "row", 1), "col", 2)
     xhat, normed, rstd = conv_norm(padded, dw_weight, layer_norm_gain)
     centered_scaled_input = xhat.reshape(total_rows, width)
     normalized_input = normed.reshape(total_rows, width)
@@ -324,38 +277,48 @@
     ).astype(jnp.bfloat16)
     g_conv4 = convolution_gradient.reshape(batch, tile_h, tile_w, width)
     w_in_term = jnp.dot(normalized_input.T, g_pre, preferred_element_type=jnp.float32).astype(jnp.bfloat16)
-    w_in_share = Halving(w_in_term, steps_of("dp", "row", "col"))
+    w_in_share = Halving(w_in_term, steps_of("dp", "col", "row"))
     g_tall = extend_along(g_conv4, "row", 1)
     first_half = kernel_gradient(padded, after(g_conv4, w_in_term), 0, 2)
+    w_in_share.part = after(w_in_share.step(), first_half)
     second_half = kernel_gradient(
-        padded, after(g_conv4, first_half, g_tall, w_in_share.step()), 1, 2
+        padded, after(g_conv4, first_half, g_tall, w_in_share.part, w_out_share.step()), 1, 2
     )
     g_padded = extend_along(g_tall, "col", 2)
     dw_term = jnp.concatenate([first_half, second_half], axis=1)
     taps = KERNEL * KERNEL
     small = jnp.concatenate([dw_term, gain_contribution[None], gamma_term[None]], axis=0)
-    columns = lax.axis_size("col")
-    padding = -small.shape[0] % (8 * columns)
-    small = jnp.pad(small, ((0, padding), (0, 0)))
+    bits = [
+        (axis, bit)
+        for axis in ("col", "dp", "row")
+        for bit in range(int(math.log2(lax.axis_size(axis))))
+    ]
     flipped = dw_weight.reshape(KERNEL, KERNEL, width)[::-1, ::-1].reshape(KERNEL * KERNEL, width)
     images = jnp.float32(batch * lax.axis_size("dp"))
     front = batch // 2
-    small = scatter_sum(small, "col")
+    small = doubled(small, *bits[0])
     part = conv_back(
-        after(g_padded, second_half, w_out_share.step()), flipped, out_grad, 0, front, None
-    )
-    w_in_second, w_out_third = w_in_share.step(), w_out_share.step()
+        after(g_padded, second_half, w_in_share.step(), small),
+        flipped,
+        out_grad,
+        0,
+        front,
+        None,
+    )
+    small = doubled(small, *bits[1])
     grad_input = conv_back(
         g_padded,
         flipped,
         out_grad,
         front,
         batch - front,
-        after(part, small, w_in_second, w_out_third),
-    )
-    small = ordered_sum(after(small, part), "row")
-    small = ordered_sum(after(small, grad_input), "dp")
-    small = jnp.concatenate(collected(small, "col"), axis=0) / images
+        after(part, small, w_in_share.step(), w_out_share.step()),
+    )
+    small = doubled(after(small, part), *bits[2])
+    small = after(small, grad_input)
+    for axis, bit in bits[3:]:
+        small = doubled(small, axis, bit)
+    small = small / images
     dw_sum, gain_sum, gamma_sum = small[:taps], small[taps], small[taps + 1]
     w_out_sum, w_in_sum = w_out_share.finish(), w_in_share.finish()
     return (

time: 256 us -> 221 us (0.86)
  Pallas kernels: 72.4 us -> 62.5 us
  waiting for transfers between devices: 40.1 us -> 31.6 us
  starting transfers between devices: 57.6 us -> 51.5 us
  local copies, waits for them, and re-layouts: 22.6 us -> 17.8 us
  other arithmetic: 16.4 us -> 12.5 us
    ppermute x10, waiting for transfers between devices: 27 us -> 0.61 us  [step(): got = lax.ppermute(theirs.astype(jnp.bfloat16), name, swap)]
    ppermute x18 -> x5, starting transfers between devices: 33.5 us -> 11.9 us  [doubled(): lax.ppermute(rows, axis, [(k, k ^ 1 << bit) for k in range(count)])]
    pallas_call x1, Pallas kernels: 30.7 us -> 20.9 us  [conv_norm(): pl.pallas_call(norm_kernel, grid=(batch, width // LANES), in_specs=[pl.Bl...]
    ppermute x18 -> x5, waiting for transfers between devices: 13.1 us -> 21.6 us  [doubled(): lax.ppermute(rows, axis, [(k, k ^ 1 << bit) for k in range(count)])]
    ppermute x10, starting transfers between devices: 11.5 us -> 19.1 us  [step(): got = lax.ppermute(theirs.astype(jnp.bfloat16), name, swap)]
    ppermute x2 -> x4, waiting for transfers between devices: 0.01 us -> 7.04 us  [extend_along(): lax.ppermute(lax.slice_in_dim(field, full - width, None, axis=dim), axis,...]
    slice x3 -> x0, local copies, waits for them, and re-layouts: 5.5 us -> none  [extend(): part = lax.slice_in_dim(part, full - width, None, axis=dim)]
    ppermute x2 -> x4, starting transfers between devices: 10 us -> 15.3 us  [extend_along(): lax.ppermute(lax.slice_in_dim(field, full - width, None, axis=dim), axis,...]
  transfers between devices with their start and end apart: 32 -> 23, of which waited for: 9 -> 7; matrix products, arithmetic and copies ran while one was open for 20% -> 18% of each run, Pallas kernels for 16% -> 19%
where the time goes in v3:
time: 221 us; the launch traced here: 220 us
  Pallas kernels  62.5 us (28%)
  starting transfers between devices  51.5 us (23%)
  matrix products  42.9 us (19%)
  waiting for transfers between devices  31.6 us (14%)
  local copies, waits for them, and re-layouts  17.8 us (8%)
  other arithmetic  12.5 us (6%)
    ppermute x5, waiting for transfers between devices, doubled(): lax.ppermute(rows, axis, [(k, k ^ 1 << bit) for k in range(count)])  21.6 us
    pallas_call x2, Pallas kernels, conv_back(): pl.pallas_call(back_kernel, grid=(width // LANES, count), in_specs=in_spe...  21 us
    pallas_call x1, Pallas kernels, conv_norm(): pl.pallas_call(norm_kernel, grid=(batch, width // LANES), in_specs=[pl.Bl...  20.9 us
    pallas_call x2, Pallas kernels, kernel_gradient(): pl.pallas_call(dw_kernel, grid=(blocks, batch), in_specs=[pl.BlockSpec((1...  20.6 us
    ppermute x10, starting transfers between devices, step(): got = lax.ppermute(theirs.astype(jnp.bfloat16), name, swap)  19.1 us
    ppermute x4, starting transfers between devices, extend_along(): lax.ppermute(lax.slice_in_dim(field, full - width, None, axis=dim), axis,...  15.3 us
    ppermute x5, starting transfers between devices, doubled(): lax.ppermute(rows, axis, [(k, k ^ 1 << bit) for k in range(count)])  11.9 us
    dot_general x1, matrix products, shards(): pre = jnp.dot(normalized_input, w_in, preferred_element_type=jnp.float32)  9.04 us
  transfers between devices with their start and end apart: 23, of which 7 were waited for; matrix products, arithmetic and copies ran while one was open for 18% of the time, Pallas kernels for 19%

profile of v3, /device:TPU:0, one launch (start us, length us, event | category | flops | bytes accessed | tf_op | source)
XLA Modules:
  0.0 220.2 jit_solution(17619110938792225790)
XLA Ops:
  1.8 5.0 %collective-permute-start = (bf16[4,3,16,1024]{3,2,1,0:T(8,128)(2,1)S(1)}, bf16[4,3,16,1024]{3,2,1,0:T(8,128)(2,1)S(1)}, u32[]{:S(2)}, u32[]{:S(2)}) collective-permute-start(bf16[4,3,16,1024]{3,2,1,0:T(8,128)(2,1)S(1)} %get-tuple-element.48), channel_id=1, source_target_pairs={{0,4},{4,8},{8,12},{1,5},{5,9},{9,13},{2,6},{6,10},{10,14},{3,7},{... | collective-permute-start | bytes 1179656 | tf_op jit(solution)/shard_map/ppermute | solution.py:21
  8.1 7.0 %collective-permute-done = bf16[4,3,16,1024]{3,2,1,0:T(8,128)(2,1)S(1)} collective-permute-done((bf16[4,3,16,1024]{3,2,1,0:T(8,128)(2,1)S(1)}, bf16[4,3,16,1024]{3,2,1,0:T(8,128)(2,1)S(1)}, u32[]{:S(2)}, u32[]{:S(2)}) %collective-permute-start) | collective-permute-done | bytes 393248 | tf_op jit(solution)/shard_map/ppermute | solution.py:21
  15.1 1.8 constant_dynamic-update-slice_fusion.1
  16.9 2.3 %collective-permute-done.1 = bf16[4,3,16,1024]{3,2,1,0:T(8,128)(2,1)S(1)} collective-permute-done((bf16[4,3,16,1024]{3,2,1,0:T(8,128)(2,1)S(1)}, bf16[4,3,16,1024]{3,2,1,0:T(8,128)(2,1)S(1)}, u32[]{:S(2)}, u32[]{:S(2)}) %collective-permute-start.1) | collective-permute-done | bytes 393248 | tf_op jit(solution)/shard_map/ppermute | solution.py:22
  23.8 3.8 %collective-permute-start.2 = (bf16[4,22,3,1024]{3,0,2,1:T(4,128)(2,1)}, bf16[4,22,3,1024]{3,0,2,1:T(4,128)(2,1)}, u32[]{:S(2)}, u32[]{:S(2)}) collective-permute-start(bf16[4,22,3,1024]{3,0,2,1:T(4,128)(2,1)} %copy.20), channel_id=1, source_target_pairs={{0,1},{1,2},{2,3},{4,5},{5,6},{6,7},{8,9},{9,10},{10,11},{12,13},{... | collective-permute-start | bytes 1622024 | tf_op jit(solution)/shard_map/ppermute | solution.py:21
  31.2 2.7 %pad_maximum_fusion.x_ref = bf16[4,22,22,1024]{3,2,1,0:T(8,128)(2,1)S(1)} fusion(bf16[4,22,3,1024]{3,2,1,0:T(4,128)(2,1)S(1)} %copy.23, bf16[4,22,16,1024]{3,2,1,0:T(8,128)(2,1)S(1)} %constant_dynamic-update-slice_fusion, bf16[4,22,3,1024]{3,2,1,0:T(4,128)(2,1)S(1)} %copy.22), kind=kLoop, calls=%fused_computation.12 | loop fusion | flops 11894784 | bytes 7929856 | tf_op jit(solution)/shard_map/concatenate | solution.py:23
  33.9 20.9 %shard_map.135 = (f32[4,16,16,1024]{3,2,1,0:T(8,128)S(1)}, bf16[4,16,16,1024]{3,2,1,0:T(8,128)(2,1)S(1)}, f32[4,16,16,1]{3,2,1,0:T(8,128)S(1)}) custom-call(bf16[4,22,22,1024]{3,2,1,0:T(8,128)(2,1)S(1)} %pad_maximum_fusion.x_ref, f32[49,1024]{1,0:T(8,128)S(1)} %convert_element_type.172.w_ref, f32[1,1024]{1,0:T(1,128)S(1)} %bitcast.86), custom_call_target="tpu_custom_call" | custom-call | flops 15728640000 | bytes 8388608 | tf_op jit(solution)/shard_map/pallas_call | solution.py:86
  54.8 1.9 copy-done.1
  57.1 9.0 %multiply_convert_fusion = (bf16[1024,2048]{1,0:T(8,128)(2,1)S(1)}, f32[1024,2048]{1,0:T(8,128)}) fusion(bf16[1024,1024]{1,0:T(8,128)(2,1)S(1)} %bitcast.87, bf16[1024,2048]{1,0:T(8,128)(2,1)} %param.12), kind=kOutput, calls=%fused_computation.7 | convolution fusion | flops 4305453056 | bytes 18874368 | tf_op jit(solution)/shard_map/dot_general | solution.py:250
  66.1 6.7 %fusion.7 = (f32[1024]{0:T(1024)S(1)}, bf16[1024,1024]{1,0:T(8,128)(2,1)}, bf16[1024,1024]{1,0:T(8,128)(2,1)S(1)}) fusion(bf16[4,16,16,1024]{3,2,1,0:T(8,128)(2,1)S(1)} %copy-done.4, f32[1024]{0:T(1024)S(1)} %bitcast.102, f32[1024]{0:T(1024)S(1)} %copy-done.9, bf16[4,16,16,1024]{3,2,1,0:T(8,128)(2,1)S(1)} %copy-done.5, ...), kind=kOutput, calls=%fused_computation.15 | convolution fusion | flops 4306500608 | bytes 16789504 | tf_op jit(solution)/shard_map/dot_general | solution.py:253
  72.9 4.9 %convolution_convert_fusion.1 = bf16[2048,1024]{1,0:T(8,128)(2,1)S(1)} fusion(bf16[1024,2048]{1,0:T(8,128)(2,1)S(1)} %get-tuple-element.51, bf16[1024,1024]{1,0:T(8,128)(2,1)S(1)} %get-tuple-element.21), kind=kOutput, calls=%fused_computation.32 | convolution fusion | flops 4297064448 | bytes 10485760 | tf_op jit(solution)/shard_map/dot_general | solution.py:259
  78.7 4.9 %collective-permute-start.4 = (bf16[2,4,2,64,1024]{4,3,1,0,2:T(8,128)(2,1)S(1)}, bf16[2,4,2,64,1024]{4,3,1,0,2:T(8,128)(2,1)S(1)}, u32[]{:S(2)}, u32[]{:S(2)}) collective-permute-start(bf16[2,4,2,64,1024]{4,3,1,0,2:T(8,128)(2,1)S(1)} %bitcast.94), channel_id=1, source_target_pairs={{0,1},{1,0},{2,3},{3,2},{4,5},{5,4},{6,7},{7,6},{8,9},{9,8},{10,11... | collective-permute-start | bytes 6291464 | tf_op jit(solution)/shard_map/ppermute | solution.py:216
  83.6 8.8 %fusion.5 = bf16[1024,2048]{1,0:T(8,128)(2,1)S(1)} fusion(f32[1024,2048]{1,0:T(8,128)} %get-tuple-element.52, bf16[1024,1024]{1,0:T(8,128)(2,1)S(1)} %get-tuple-element.21, bf16[2048,1024]{1,0:T(8,128)(2,1)S(1)} %copy-done.8), kind=kOutput, calls=%fused_computation.6 | convolution fusion | flops 4315938816 | bytes 18874368 | tf_op jit(solution)/shard_map/dot_general | solution.py:263
  92.5 4.9 %convolution_convert_fusion = bf16[1024,2048]{1,0:T(8,128)(2,1)S(1)} fusion(bf16[1024,1024]{1,0:T(8,128)(2,1)S(1)} %bitcast.88, bf16[1024,2048]{1,0:T(8,128)(2,1)S(1)} %fusion.5), kind=kOutput, calls=%fused_computation.31 | convolution fusion | flops 4297064448 | bytes 10485760 | tf_op jit(solution)/shard_map/dot_general | solution.py:279
  100.4 8.5 %fusion.17 = (f32[1024]{0:T(1024)S(1)}, f32[1024]{0:T(1024)S(1)}, f32[1024]{0:T(1024)S(1)}, f32[1024,1024]{1,0:T(8,128)S(1)}) fusion(f32[4,16,16,1024]{3,2,1,0:T(8,128)S(1)} %copy-done.2, f32[1024]{0:T(1024)S(1)} %copy-done.3, bf16[1024,2048]{1,0:T(8,128)(2,1)} %copy-done.11, bf16[1024,2048]{1,0:T(8,128)(2,1)} %param.12), kind=kOutput, calls=%fused_computation.30 | convolution fusion | flops 4301255680 | bytes 16793600 | tf_op jit(solution)/shard_map/dot_general | solution.py:266
  110.5 3.5 %collective-permute-start.5 = (bf16[4,3,16,1024]{3,2,1,0:T(8,128)(2,1)S(1)}, bf16[4,3,16,1024]{3,2,1,0:T(8,128)(2,1)S(1)}, u32[]{:S(2)}, u32[]{:S(2)}) collective-permute-start(bf16[4,3,16,1024]{3,2,1,0:T(8,128)(2,1)S(1)} %get-tuple-element.45), channel_id=1, source_target_pairs={{0,4},{4,8},{8,12},{1,5},{5,9},{9,13},{2,6},{6,10},{10,14},{3,7},{... | collective-permute-start | bytes 1179656 | tf_op jit(solution)/shard_map/ppermute | solution.py:21
  115.4 2.7 %collective-permute-start.10 = (bf16[2,4,1,64,1024]{4,3,1,0,2:T(8,128)(2,1)S(1)}, bf16[2,4,1,64,1024]{4,3,1,0,2:T(8,128)(2,1)S(1)}, u32[]{:S(2)}, u32[]{:S(2)}) collective-permute-start(bf16[2,4,1,64,1024]{4,3,1,0,2:T(8,128)(2,1)S(1)} %constant_dynamic-slice_fusion.5), channel_id=1, source_target_pairs={{0,2},{1,3},{2,0},{3,1},{4,6},{5,7},{6,4},{7,5},{8,10},{9,11},{10,... | collective-permute-start | bytes 3145736 | tf_op jit(solution)/shard_map/ppermute | solution.py:216
  118.1 10.3 %shard_map.136 = f32[49,512]{1,0:T(8,128)S(1)} custom-call(bf16[4,22,22,1024]{3,2,1,0:T(8,128)(2,1)S(1)} %bitcast.85, bf16[4,16,16,1024]{3,2,1,0:T(8,128)(2,1)S(1)} %bitcast.80), custom_call_target="tpu_custom_call" | custom-call | flops 7864320000 | bytes 3145728 | tf_op jit(solution)/shard_map/pallas_call | solution.py:177
  131.8 3.1 %collective-permute-start.7 = (bf16[4,22,3,1024]{3,0,2,1:T(4,128)(2,1)S(1)}, bf16[4,22,3,1024]{3,0,2,1:T(4,128)(2,1)S(1)}, u32[]{:S(2)}, u32[]{:S(2)}) collective-permute-start(bf16[4,22,3,1024]{3,0,2,1:T(4,128)(2,1)S(1)} %copy.26), channel_id=1, source_target_pairs={{0,1},{1,2},{2,3},{4,5},{5,6},{6,7},{8,9},{9,10},{10,11},{12,13},{... | collective-permute-start | bytes 1622024 | tf_op jit(solution)/shard_map/ppermute | solution.py:21
  135.8 1.6 collective-permute-start.11
  138.1 3.0 %pad_maximum_fusion.1.x_ref = bf16[4,22,22,1024]{3,2,1,0:T(8,128)(2,1)S(1)} fusion(bf16[4,22,3,1024]{3,2,1,0:T(4,128)(2,1)S(1)} %copy.29, bf16[4,3,16,1024]{3,2,1,0:T(8,128)(2,1)S(1)} %collective-permute-done.6, bf16[4,16,16,1024]{3,2,1,0:T(8,128)(2,1)S(1)} %bitcast.82, bf16[4,3,16,1024]{3,2,1,0:T(8,128)(2,1)S(1)} %collective-permute-done.5, ...), kind=kLoop, calls=%fused_computation.13 | loop fusion | flops 19824640 | bytes 7929856 | tf_op jit(solution)/shard_map/concatenate | solution.py:23
  142.1 2.7 %collective-permute-start.15 = (bf16[2,2,1,64,1024]{4,3,1,0,2:T(8,128)(2,1)S(1)}, bf16[2,2,1,64,1024]{4,3,1,0,2:T(8,128)(2,1)S(1)}, u32[]{:S(2)}, u32[]{:S(2)}) collective-permute-start(bf16[2,2,1,64,1024]{4,3,1,0,2:T(8,128)(2,1)S(1)} %dynamic-slice_bitcast_fusion), channel_id=1, source_target_pairs={{0,4},{4,0},{8,12},{12,8},{1,5},{5,1},{9,13},{13,9},{2,6},{6,2},{1... | collective-permute-start | bytes 1572872 | tf_op jit(solution)/shard_map/ppermute | solution.py:216
  144.8 10.3 %shard_map.137 = f32[49,512]{1,0:T(8,128)S(1)} custom-call(bf16[4,22,22,1024]{3,2,1,0:T(8,128)(2,1)S(1)} %bitcast.85, bf16[4,16,16,1024]{3,2,1,0:T(8,128)(2,1)S(1)} %bitcast.83), custom_call_target="tpu_custom_call" | custom-call | flops 7864320000 | bytes 3145728 | tf_op jit(solution)/shard_map/pallas_call | solution.py:177
  155.2 8.9 %collective-permute-start.12 = (f32[51,1024]{1,0:T(8,128)S(1)}, f32[51,1024]{1,0:T(8,128)S(1)}, u32[]{:S(2)}, u32[]{:S(2)}) collective-permute-start(f32[51,1024]{1,0:T(8,128)S(1)} %pad_maximum_fusion.3), channel_id=1, source_target_pairs={{0,1},{1,0},{2,3},{3,2},{4,5},{5,4},{6,7},{7,6},{8,9},{9,8},{10,11... | collective-permute-start | bytes 626696 | tf_op jit(solution)/shard_map/ppermute | solution.py:229
  164.6 1.6 collective-permute-start.14
  167.2 10.5 %shard_map.138.rest_0_ = bf16[4,16,16,1024]{3,2,1,0:T(8,128)(2,1)} custom-call(bf16[4,22,22,1024]{3,2,1,0:T(8,128)(2,1)S(1)} %pad_maximum_fusion.1.x_ref, f32[49,1024]{1,0:T(8,128)S(1)} %reshape.147.w_ref, bf16[4,16,16,1024]{3,2,1,0:T(8,128)(2,1)S(1)} %copy-done.4), custom_call_target="tpu_custom_call" | custom-call | flops 7864320000 | bytes 3145728 | tf_op jit(solution)/shard_map/pallas_call | solution.py:135
  177.7 6.0 %collective-permute-done.13 = f32[51,1024]{1,0:T(8,128)S(1)} collective-permute-done((f32[51,1024]{1,0:T(8,128)S(1)}, f32[51,1024]{1,0:T(8,128)S(1)}, u32[]{:S(2)}, u32[]{:S(2)}) %collective-permute-start.13) | collective-permute-done | bytes 208928 | tf_op jit(solution)/shard_map/ppermute | solution.py:229
  187.1 1.8 collective-permute-start.16
  188.9 10.5 %shard_map.139 = bf16[4,16,16,1024]{3,2,1,0:T(8,128)(2,1)} custom-call(bf16[4,22,22,1024]{3,2,1,0:T(8,128)(2,1)S(1)} %pad_maximum_fusion.1.x_ref, f32[49,1024]{1,0:T(8,128)S(1)} %reshape.147.w_ref, bf16[4,16,16,1024]{3,2,1,0:T(8,128)(2,1)S(1)} %copy-done.4, bf16[4,16,16,1024]{3,2,1,0:T(8,128)(2,1)} %shard_map.138.rest_0_), custom_call_target="tpu_custom_call", output_to_operand_aliasing={{}: (3, {})} | custom-call | flops 7864320000 | bytes 3145728 | tf_op jit(solution)/shard_map/pallas_call | solution.py:135
  199.9 1.6 collective-permute-start.17
  202.2 6.2 %collective-permute-done.21 = f32[51,1024]{1,0:T(8,128)S(1)} collective-permute-done((f32[51,1024]{1,0:T(8,128)S(1)}, f32[51,1024]{1,0:T(8,128)S(1)}, u32[]{:S(2)}, u32[]{:S(2)}) %collective-permute-start.21) | collective-permute-done | bytes 208928 | tf_op jit(solution)/shard_map/ppermute | solution.py:229
  210.0 9.5 %collective-permute-done.22 = f32[51,1024]{1,0:T(8,128)S(1)} collective-permute-done((f32[51,1024]{1,0:T(8,128)S(1)}, f32[51,1024]{1,0:T(8,128)S(1)}, u32[]{:S(2)}, u32[]{:S(2)}) %collective-permute-start.22) | collective-permute-done | bytes 208928 | tf_op jit(solution)/shard_map/ppermute | solution.py:229
  (112 shorter events, 32.0 us)
Async XLA Ops:
  1.8 13.3 %collective-permute-start = (bf16[4,3,16,1024]{3,2,1,0:T(8,128)(2,1)S(1)}, bf16[4,3,16,1024]{3,2,1,0:T(8,128)(2,1)S(1)}, u32[]{:S(2)}, u32[]{:S(2)}) collective-permute-start(bf16[4,3,16,1024]{3,2,1,0:T(8,128)(2,1)S(1)} %get-tuple-element.48), channel_id=1, source_target_pairs={{0,4},{4,8},{8,12},{1,5},{5,9},{9,13},{2,6},{6,10},{10,14},{3,7},{... | collective-permute-start | bytes 1179656 | tf_op jit(solution)/shard_map/ppermute | solution.py:21
  6.8 12.5 %collective-permute-start.1 = (bf16[4,3,16,1024]{3,2,1,0:T(8,128)(2,1)S(1)}, bf16[4,3,16,1024]{3,2,1,0:T(8,128)(2,1)S(1)}, u32[]{:S(2)}, u32[]{:S(2)}) collective-permute-start(bf16[4,3,16,1024]{3,2,1,0:T(8,128)(2,1)S(1)} %get-tuple-element.47), channel_id=1, source_target_pairs={{4,0},{8,4},{12,8},{5,1},{9,5},{13,9},{6,2},{10,6},{14,10},{7,3},{... | collective-permute-start | bytes 1179656 | tf_op jit(solution)/shard_map/ppermute | solution.py:22
  16.9 10.8 %copy-start.6 = (bf16[49,1024]{1,0:T(8,128)(2,1)S(1)}, bf16[49,1024]{1,0:T(8,128)(2,1)}, u32[]{:S(2)}) copy-start(bf16[49,1024]{1,0:T(8,128)(2,1)} %param.10) | copy-start | bytes 301060
  16.9 10.8 %copy-start.10 = (s32[4]{0:T(128)S(1)}, s32[4]{0:T(128)}, u32[]{:S(2)}) copy-start(s32[4]{0:T(128)} %param.9) | copy-start | bytes 52
  21.2 7.1 %collective-permute-start.3 = (bf16[4,22,3,1024]{3,0,2,1:T(4,128)(2,1)}, bf16[4,22,3,1024]{3,0,2,1:T(4,128)(2,1)}, u32[]{:S(2)}, u32[]{:S(2)}) collective-permute-start(bf16[4,22,3,1024]{3,0,2,1:T(4,128)(2,1)} %copy.21), channel_id=1, source_target_pairs={{1,0},{2,1},{3,2},{5,4},{6,5},{7,6},{9,8},{10,9},{11,10},{13,12},{... | collective-permute-start | bytes 1622024 | tf_op jit(solution)/shard_map/ppermute | solution.py:22
  23.8 5.9 %collective-permute-start.2 = (bf16[4,22,3,1024]{3,0,2,1:T(4,128)(2,1)}, bf16[4,22,3,1024]{3,0,2,1:T(4,128)(2,1)}, u32[]{:S(2)}, u32[]{:S(2)}) collective-permute-start(bf16[4,22,3,1024]{3,0,2,1:T(4,128)(2,1)} %copy.20), channel_id=1, source_target_pairs={{0,1},{1,2},{2,3},{4,5},{5,6},{6,7},{8,9},{9,10},{10,11},{12,13},{... | collective-permute-start | bytes 1622024 | tf_op jit(solution)/shard_map/ppermute | solution.py:21
  33.9 20.9 %copy-start = (bf16[4,22,22,1024]{3,2,1,0:T(8,128)(2,1)}, bf16[4,22,22,1024]{3,2,1,0:T(8,128)(2,1)S(1)}, u32[]{:S(2)}) copy-start(bf16[4,22,22,1024]{3,2,1,0:T(8,128)(2,1)S(1)} %pad_maximum_fusion.x_ref) | copy-start | bytes 11894788
  57.0 9.1 %copy-start.4 = (bf16[4,16,16,1024]{3,2,1,0:T(8,128)(2,1)S(1)}, bf16[4,16,16,1024]{3,2,1,0:T(8,128)(2,1)}, u32[]{:S(2)}) copy-start(bf16[4,16,16,1024]{3,2,1,0:T(8,128)(2,1)} %extra_ref.3) | copy-start | bytes 6291460
  57.0 9.1 %copy-start.5 = (bf16[4,16,16,1024]{3,2,1,0:T(8,128)(2,1)S(1)}, bf16[4,16,16,1024]{3,2,1,0:T(8,128)(2,1)}, u32[]{:S(2)}) copy-start(bf16[4,16,16,1024]{3,2,1,0:T(8,128)(2,1)} %param.8) | copy-start | bytes 6291460
  57.1 9.1 %copy-start.8 = (bf16[2048,1024]{1,0:T(8,128)(2,1)S(1)}, bf16[2048,1024]{1,0:T(8,128)(2,1)}, u32[]{:S(2)}) copy-start(bf16[2048,1024]{1,0:T(8,128)(2,1)} %param.13) | copy-start | bytes 12582916
  57.1 9.1 %copy-start.9 = (f32[1024]{0:T(1024)S(1)}, f32[1024]{0:T(1024)}, u32[]{:S(2)}) copy-start(f32[1024]{0:T(1024)} %param.14) | copy-start | bytes 12292
  78.7 19.8 %collective-permute-start.4 = (bf16[2,4,2,64,1024]{4,3,1,0,2:T(8,128)(2,1)S(1)}, bf16[2,4,2,64,1024]{4,3,1,0,2:T(8,128)(2,1)S(1)}, u32[]{:S(2)}, u32[]{:S(2)}) collective-permute-start(bf16[2,4,2,64,1024]{4,3,1,0,2:T(8,128)(2,1)S(1)} %bitcast.94), channel_id=1, source_target_pairs={{0,1},{1,0},{2,3},{3,2},{4,5},{5,4},{6,7},{7,6},{8,9},{9,8},{10,11... | collective-permute-start | bytes 6291464 | tf_op jit(solution)/shard_map/ppermute | solution.py:216
  98.2 36.6 %collective-permute-start.9 = (bf16[2,4,2,32,2048]{4,3,1,2,0:T(8,128)(2,1)S(1)}, bf16[2,4,2,32,2048]{4,3,1,2,0:T(8,128)(2,1)S(1)}, u32[]{:S(2)}, u32[]{:S(2)}) collective-permute-start(bf16[2,4,2,32,2048]{4,3,1,2,0:T(8,128)(2,1)S(1)} %bitcast.93), channel_id=1, source_target_pairs={{0,1},{1,0},{2,3},{3,2},{4,5},{5,4},{6,7},{7,6},{8,9},{9,8},{10,11... | collective-permute-start | bytes 6291464 | tf_op jit(solution)/shard_map/ppermute | solution.py:216
  98.5 19.5 %slice-start = ((s8[4325376]{0:T(1024)(128)(4,1)}), s8[4194304]{0:T(1024)(128)(4,1)S(1)}, s32[]{:S(2)}) async-start(s8[4325376]{0:T(1024)(128)(4,1)} %bitcast.84), calls=%async_computation | async-start | bytes 8388608
  100.4 17.7 %slice-start.1 = ((s8[4325376]{0:T(1024)(128)(4,1)}), s8[131072]{0:T(1024)(128)(4,1)S(1)}, s32[]{:S(2)}) async-start(s8[4325376]{0:T(1024)(128)(4,1)} %bitcast.84), calls=%async_computation.1 | async-start | bytes 262144
  110.5 17.9 %collective-permute-start.5 = (bf16[4,3,16,1024]{3,2,1,0:T(8,128)(2,1)S(1)}, bf16[4,3,16,1024]{3,2,1,0:T(8,128)(2,1)S(1)}, u32[]{:S(2)}, u32[]{:S(2)}) collective-permute-start(bf16[4,3,16,1024]{3,2,1,0:T(8,128)(2,1)S(1)} %get-tuple-element.45), channel_id=1, source_target_pairs={{0,4},{4,8},{8,12},{1,5},{5,9},{9,13},{2,6},{6,10},{10,14},{3,7},{... | collective-permute-start | bytes 1179656 | tf_op jit(solution)/shard_map/ppermute | solution.py:21
  114.0 14.4 %collective-permute-start.6 = (bf16[4,3,16,1024]{3,2,1,0:T(8,128)(2,1)S(1)}, bf16[4,3,16,1024]{3,2,1,0:T(8,128)(2,1)S(1)}, u32[]{:S(2)}, u32[]{:S(2)}) collective-permute-start(bf16[4,3,16,1024]{3,2,1,0:T(8,128)(2,1)S(1)} %get-tuple-element.46), channel_id=1, source_target_pairs={{4,0},{8,4},{12,8},{5,1},{9,5},{13,9},{6,2},{10,6},{14,10},{7,3},{... | collective-permute-start | bytes 1179656 | tf_op jit(solution)/shard_map/ppermute | solution.py:22
  115.4 26.2 %collective-permute-start.10 = (bf16[2,4,1,64,1024]{4,3,1,0,2:T(8,128)(2,1)S(1)}, bf16[2,4,1,64,1024]{4,3,1,0,2:T(8,128)(2,1)S(1)}, u32[]{:S(2)}, u32[]{:S(2)}) collective-permute-start(bf16[2,4,1,64,1024]{4,3,1,0,2:T(8,128)(2,1)S(1)} %constant_dynamic-slice_fusion.5), channel_id=1, source_target_pairs={{0,2},{1,3},{2,0},{3,1},{4,6},{5,7},{6,4},{7,5},{8,10},{9,11},{10,... | collective-permute-start | bytes 3145736 | tf_op jit(solution)/shard_map/ppermute | solution.py:216
  130.5 6.9 %collective-permute-start.8 = (bf16[4,22,3,1024]{3,0,2,1:T(4,128)(2,1)S(1)}, bf16[4,22,3,1024]{3,0,2,1:T(4,128)(2,1)S(1)}, u32[]{:S(2)}, u32[]{:S(2)}) collective-permute-start(bf16[4,22,3,1024]{3,0,2,1:T(4,128)(2,1)S(1)} %copy.27), channel_id=1, source_target_pairs={{1,0},{2,1},{3,2},{5,4},{6,5},{7,6},{9,8},{10,9},{11,10},{13,12},{... | collective-permute-start | bytes 1622024 | tf_op jit(solution)/shard_map/ppermute | solution.py:22
  131.8 6.0 %collective-permute-start.7 = (bf16[4,22,3,1024]{3,0,2,1:T(4,128)(2,1)S(1)}, bf16[4,22,3,1024]{3,0,2,1:T(4,128)(2,1)S(1)}, u32[]{:S(2)}, u32[]{:S(2)}) collective-permute-start(bf16[4,22,3,1024]{3,0,2,1:T(4,128)(2,1)S(1)} %copy.26), channel_id=1, source_target_pairs={{0,1},{1,2},{2,3},{4,5},{5,6},{6,7},{8,9},{9,10},{10,11},{12,13},{... | collective-permute-start | bytes 1622024 | tf_op jit(solution)/shard_map/ppermute | solution.py:21
  135.8 28.3 %collective-permute-start.11 = (bf16[1,4,2,32,2048]{4,3,1,2,0:T(8,128)(2,1)S(1)}, bf16[1,4,2,32,2048]{4,3,1,2,0:T(8,128)(2,1)S(1)}, u32[]{:S(2)}, u32[]{:S(2)}) collective-permute-start(bf16[1,4,2,32,2048]{4,3,1,2,0:T(8,128)(2,1)S(1)} %constant_dynamic-slice_fusion.4), channel_id=1, source_target_pairs={{0,16},{16,0},{1,17},{17,1},{2,18},{18,2},{3,19},{19,3},{4,20},{20... | collective-permute-start | bytes 3145736 | tf_op jit(solution)/shard_map/ppermute | solution.py:216
  142.1 43.2 %collective-permute-start.15 = (bf16[2,2,1,64,1024]{4,3,1,0,2:T(8,128)(2,1)S(1)}, bf16[2,2,1,64,1024]{4,3,1,0,2:T(8,128)(2,1)S(1)}, u32[]{:S(2)}, u32[]{:S(2)}) collective-permute-start(bf16[2,2,1,64,1024]{4,3,1,0,2:T(8,128)(2,1)S(1)} %dynamic-slice_bitcast_fusion), channel_id=1, source_target_pairs={{0,4},{4,0},{8,12},{12,8},{1,5},{5,1},{9,13},{13,9},{2,6},{6,2},{1... | collective-permute-start | bytes 1572872 | tf_op jit(solution)/shard_map/ppermute | solution.py:216
  155.2 11.0 %collective-permute-start.12 = (f32[51,1024]{1,0:T(8,128)S(1)}, f32[51,1024]{1,0:T(8,128)S(1)}, u32[]{:S(2)}, u32[]{:S(2)}) collective-permute-start(f32[51,1024]{1,0:T(8,128)S(1)} %pad_maximum_fusion.3), channel_id=1, source_target_pairs={{0,1},{1,0},{2,3},{3,2},{4,5},{5,4},{6,7},{7,6},{8,9},{9,8},{10,11... | collective-permute-start | bytes 626696 | tf_op jit(solution)/shard_map/ppermute | solution.py:229
  164.6 22.3 %collective-permute-start.14 = (bf16[1,4,1,32,2048]{4,3,1,2,0:T(8,128)(2,1)S(1)}, bf16[1,4,1,32,2048]{4,3,1,2,0:T(8,128)(2,1)S(1)}, u32[]{:S(2)}, u32[]{:S(2)}) collective-permute-start(bf16[1,4,1,32,2048]{4,3,1,2,0:T(8,128)(2,1)S(1)} %constant_dynamic-slice_fusion.3), channel_id=1, source_target_pairs={{0,2},{1,3},{2,0},{3,1},{4,6},{5,7},{6,4},{7,5},{8,10},{9,11},{10,... | collective-permute-start | bytes 1572872 | tf_op jit(solution)/shard_map/ppermute | solution.py:216
  166.2 17.4 %collective-permute-start.13 = (f32[51,1024]{1,0:T(8,128)S(1)}, f32[51,1024]{1,0:T(8,128)S(1)}, u32[]{:S(2)}, u32[]{:S(2)}) collective-permute-start(f32[51,1024]{1,0:T(8,128)S(1)} %fusion.37), channel_id=1, source_target_pairs={{0,2},{1,3},{2,0},{3,1},{4,6},{5,7},{6,4},{7,5},{8,10},{9,11},{10,... | collective-permute-start | bytes 626696 | tf_op jit(solution)/shard_map/ppermute | solution.py:229
  183.7 15.7 %collective-permute-start.20 = (f32[51,1024]{1,0:T(8,128)S(1)}, f32[51,1024]{1,0:T(8,128)S(1)}, u32[]{:S(2)}, u32[]{:S(2)}) collective-permute-start(f32[51,1024]{1,0:T(8,128)S(1)} %add.156), channel_id=1, source_target_pairs={{0,16},{16,0},{1,17},{17,1},{2,18},{18,2},{3,19},{19,3},{4,20},{20... | collective-permute-start | bytes 626696 | tf_op jit(solution)/shard_map/ppermute | solution.py:229
  185.5 16.0 %collective-permute-start.18 = (bf16[2,1,1,64,1024]{4,3,1,0,2:T(8,128)(2,1)S(1)}, bf16[2,1,1,64,1024]{4,3,1,0,2:T(8,128)(2,1)S(1)}, u32[]{:S(2)}, u32[]{:S(2)}) collective-permute-start(bf16[2,1,1,64,1024]{4,3,1,0,2:T(8,128)(2,1)S(1)} %constant_dynamic-slice_fusion.1), channel_id=1, source_target_pairs={{0,8},{4,12},{8,0},{12,4},{1,9},{5,13},{9,1},{13,5},{2,10},{6,14},... | collective-permute-start | bytes 786440 | tf_op jit(solution)/shard_map/ppermute | solution.py:216
  187.1 12.8 %collective-permute-start.16 = (bf16[1,2,1,32,2048]{4,3,1,2,0:T(8,128)(2,1)S(1)}, bf16[1,2,1,32,2048]{4,3,1,2,0:T(8,128)(2,1)S(1)}, u32[]{:S(2)}, u32[]{:S(2)}) collective-permute-start(bf16[1,2,1,32,2048]{4,3,1,2,0:T(8,128)(2,1)S(1)} %dynamic-slice_bitcast_fusion.1), channel_id=1, source_target_pairs={{0,4},{4,0},{8,12},{12,8},{1,5},{5,1},{9,13},{13,9},{2,6},{6,2},{1... | collective-permute-start | bytes 786440 | tf_op jit(solution)/shard_map/ppermute | solution.py:216
  199.4 9.0 %collective-permute-start.21 = (f32[51,1024]{1,0:T(8,128)S(1)}, f32[51,1024]{1,0:T(8,128)S(1)}, u32[]{:S(2)}, u32[]{:S(2)}) collective-permute-start(f32[51,1024]{1,0:T(8,128)S(1)} %add.169), channel_id=1, source_target_pairs={{0,4},{4,0},{8,12},{12,8},{1,5},{5,1},{9,13},{13,9},{2,6},{6,2},{1... | collective-permute-start | bytes 626696 | tf_op jit(solution)/shard_map/ppermute | solution.py:229
  199.9 8.6 %collective-permute-start.17 = (bf16[1,1,1,32,2048]{4,3,1,2,0:T(8,128)(2,1)S(1)}, bf16[1,1,1,32,2048]{4,3,1,2,0:T(8,128)(2,1)S(1)}, u32[]{:S(2)}, u32[]{:S(2)}) collective-permute-start(bf16[1,1,1,32,2048]{4,3,1,2,0:T(8,128)(2,1)S(1)} %constant_dynamic-slice_fusion.2), channel_id=1, source_target_pairs={{0,8},{4,12},{8,0},{12,4},{1,9},{5,13},{9,1},{13,5},{2,10},{6,14},... | collective-permute-start | bytes 393224 | tf_op jit(solution)/shard_map/ppermute | solution.py:216
  201.7 7.6 %collective-permute-start.19 = (bf16[1,1,1,64,1024]{4,3,1,0,2:T(8,128)(2,1)S(1)}, bf16[1,1,1,64,1024]{4,3,1,0,2:T(8,128)(2,1)S(1)}, u32[]{:S(2)}, u32[]{:S(2)}) collective-permute-start(bf16[1,1,1,64,1024]{4,3,1,0,2:T(8,128)(2,1)S(1)} %constant_dynamic-slice_fusion), channel_id=1, source_target_pairs={{0,16},{16,0},{1,17},{17,1},{2,18},{18,2},{3,19},{19,3},{4,20},{20... | collective-permute-start | bytes 393224 | tf_op jit(solution)/shard_map/ppermute | solution.py:216
  208.4 11.1 %collective-permute-start.22 = (f32[51,1024]{1,0:T(8,128)S(1)}, f32[51,1024]{1,0:T(8,128)S(1)}, u32[]{:S(2)}, u32[]{:S(2)}) collective-permute-start(f32[51,1024]{1,0:T(8,128)S(1)} %add.170), channel_id=1, source_target_pairs={{0,8},{4,12},{8,0},{12,4},{1,9},{5,13},{9,1},{13,5},{2,10},{6,14},... | collective-permute-start | bytes 626696 | tf_op jit(solution)/shard_map/ppermute | solution.py:229
  (5 other events, 12.5 us)
